TPU v7x, 256 devices: a whole 4x4x8 slice. The times are simulated.
256 devices in a mesh: lon: 32 (over z, y_hi, core), lat: 8 (over x, y_lo).
Axes of the slice: x: 4, y: 4 (y_hi: 2, y_lo: 2; y = y_hi * 2 + y_lo), z: 8, core: 2. Of those that a mesh axis runs over, the one named last changes fastest.
Arguments:
- tokens: bfloat16 [4, 64, 256, 512], P(None, 'lat', 'lon'), may hold values from -54 to 54
- cotangent: bfloat16 [4, 64, 256, 512], P(None, 'lat', 'lon'), may hold values from -6 to 6
- norm_gain: float32 [512], replicated, may hold values from 0.25 to 1.75
- w_qkv: bfloat16 [512, 1536], replicated, may hold values from -0.25 to 0.25
- w_out: bfloat16 [512, 512], replicated, may hold values from -0.25 to 0.25
Outputs:
- grad_tokens: bfloat16 [4, 64, 256, 512], P(None, 'lat', 'lon')
- grad_qkv: float32 [512, 1536], P('lon', 'lat')
- grad_out: float32 [512, 512], P('lon', 'lat')
- grad_gain: float32 [512], replicated
All inputs are finite; a program needn't handle non-finite values.
Results may differ from a plain program's by a relative error of at most 0.027.
Values may be sent and summed in bfloat16 or wider, within the bound.
No kernel may reach another device: no remote copies, remote signals or barrier semaphores. Data moves between devices by JAX's collectives and lax.ppermute only.
A program may use at most 64 MiB of HBM per device.

v0:
```python
import jax
import jax.numpy as jnp
from jax import lax
from jax.experimental import pallas as pl
from jax.experimental.pallas import tpu as pltpu
from jax.sharding import Mesh, PartitionSpec as P

HD = 32
F32 = jnp.float32
BF16 = jnp.bfloat16
LOG2E = 1.4426950408889634
QFOLD = HD ** (-0.5) * LOG2E
ROWS = 1040


def mm(a, b):
    return lax.dot_general(a, b, (((1,), (0,)), ((), ())), preferred_element_type=F32)


def mt(a, b):
    return lax.dot_general(a, b, (((1,), (1,)), ((), ())), preferred_element_type=F32)


def split2(v):
    hi = v.astype(BF16)
    return hi, (v - hi.astype(F32)).astype(BF16)


def iota(shape, dim):
    return lax.broadcasted_iota(jnp.int32, shape, dim)


def swap16(v):
    low = iota(v.shape, 1) % HD < 16
    return jnp.where(low, pltpu.roll(v, 112, 1), pltpu.roll(v, 16, 1))


def quads_kernel(x_ref, dy_ref, diag_ref, east_ref, below_ref, own_ref, buf, sems):
    copies = []
    for j, ref in enumerate((x_ref, dy_ref)):
        for w in range(4):
            copy = pltpu.make_async_copy(ref.at[w], buf.at[j, w], sems.at[j, w])
            copy.start()
            copies.append((j, w, copy))
    for j, w, copy in copies:
        copy.wait()
        t = buf[j, w]
        diag_ref[j, w] = t[:4, :4]
        east_ref[j, w] = t[4:, :4]
        below_ref[j, w] = t[:4, 4:]
        own_ref[j, w] = t[4:, 4:]


def head_ones():
    return (iota((128, 128), 0) // HD == iota((128, 128), 1) // HD).astype(F32).astype(BF16)


def forward_kernel(
    x_ref, gain_ref, wqkv_ref, cos_ref, sin_ref,
    n_ref, qk_ref, v_ref, scale_ref, qkv_ref,
):
    gain = gain_ref[...]
    for w in range(4):
        rows = slice(64 * w, 64 * w + 64)
        xs = x_ref[rows, :].astype(F32)
        inv = lax.rsqrt(jnp.mean(xs * xs, -1, keepdims=True) + 1e-05)
        n_ref[rows, :] = (xs * inv * gain).astype(BF16)
    qkv_ref[...] = mm(n_ref[...], wqkv_ref[...])
    cosine, sine, ones32 = cos_ref[...], sin_ref[...], head_ones()
    for w in range(4):
        rows = slice(64 * w, 64 * w + 64)
        tiles = [qkv_ref[rows, 128 * j : 128 * j + 128] for j in range(8)]
        squares = mm(jnp.concatenate([(t * t).astype(BF16) for t in tiles], 0), ones32)
        for j, t in enumerate(tiles):
            cut = slice(128 * j, 128 * j + 128)
            s = lax.rsqrt(squares[64 * j : 64 * j + 64] * (1.0 / HD) + 1e-06)
            scale_ref[rows, cut] = s
            factor = s * QFOLD if j < 4 else s
            qk_ref[rows, cut] = ((t * cosine + swap16(t) * sine) * factor).astype(BF16)
        v_ref[rows, :] = qkv_ref[rows, 1024:1536].astype(BF16)


def backward_kernel(
    place, x_ref, dy_ref, wqkv_ref, wout_ref, cos_ref, sin_ref, n_ref, qk_ref, v_ref, scale_ref,
    send_ref, dqkv_ref, dn_ref, nt_ref, at_ref, tail_ref,
    da_ref, att_ref,
):
    core, xpos, capped = place[0], place[1], place[2]
    da_ref[...] = mt(dy_ref[...], wout_ref[...]).astype(BF16)

    lane = iota((64, 128), 1)
    head = [(lane // HD == h).astype(F32).astype(BF16) for h in range(4)]

    def spread(t):
        return jnp.concatenate([t * head[h] for h in range(4)], axis=0)

    ones32 = head_ones()
    ones_num = (iota((256, 128), 0) // 64 == iota((256, 128), 1) // HD).astype(F32).astype(BF16)
    ones_row = (iota((256, 256), 0) % 128 // HD == iota((256, 256), 1) // 64).astype(F32).astype(BF16)
    half_a = iota((64, 256), 0) // 32
    half_b = iota((64, 256), 1) % 64 // 32
    allowed = jnp.logical_or(half_a == half_b, capped == 0)
    cosine, sine = cos_ref[...], sin_ref[...]
    groups = range(4)

    def window(w):
        rows = slice(64 * w, 64 * w + 64)
        q = [qk_ref[rows, 128 * g : 128 * g + 128] for g in groups]
        k = [qk_ref[rows, 512 + 128 * g : 512 + 128 * g + 128] for g in groups]
        v = [v_ref[rows, 128 * g : 128 * g + 128] for g in groups]
        da = [da_ref[rows, 128 * g : 128 * g + 128] for g in groups]
        qb = [spread(t) for t in q]
        kb = [spread(t) for t in k]
        vb = [spread(t) for t in v]
        db = [spread(t) for t in da]

        e = [jnp.where(allowed, jnp.exp2(mt(q[g], kb[g])), 0.0) for g in groups]
        nd = [mm(e[g].astype(BF16), jnp.concatenate([vb[g], ones_num], axis=1)) for g in groups]
        rden = [1.0 / t[:, 128:] for t in nd]
        att = [t[:, :128] * r for t, r in zip(nd, rden)]
        for g in groups:
            att_ref[rows, 128 * g : 128 * g + 128] = att[g].astype(BF16)
        dp = [mt(da[g], vb[g]) for g in groups]
        dots = [jnp.concatenate(split2(da[g].astype(F32) * att[g]), axis=1) for g in groups]
        r = mm(jnp.concatenate(dots, 0), ones_row)
        xe = [(e[g] * (dp[g] - r[64 * g : 64 * g + 64])).astype(BF16) for g in groups]
        dqr = [mm(xe[g], kb[g]) * (rden[g] * HD ** (-0.5)) for g in groups]
        et = [jnp.where(allowed, jnp.exp2(mt(k[g], qb[g])), 0.0) for g in groups]
        pt = [t * (1.0 / jnp.sum(t, 0, keepdims=True)) for t in et]
        dpt = [mt(v[g], db[g]) for g in groups]
        rt = [jnp.sum(pt[g] * dpt[g], 0, keepdims=True) for g in groups]
        dst = [(pt[g] * (dpt[g] - rt[g])).astype(BF16) for g in groups]
        dv = [mm(pt[g].astype(BF16), db[g]) for g in groups]
        dkr = [mm(dst[g], qb[g]) * (1.0 / LOG2E) for g in groups]

        grads, tiles = dqr + dkr, q + k
        dots = [(d * t.astype(F32)).astype(BF16) for d, t in zip(grads, tiles)]
        means = mm(jnp.concatenate(dots, 0), ones32)
        for j, (d, t) in enumerate(zip(grads, tiles)):
            cut = slice(128 * j, 128 * j + 128)
            m = means[64 * j : 64 * j + 64] * (1.0 / (HD * QFOLD * QFOLD) if j < 4 else 1.0 / HD)
            u = scale_ref[rows, cut] * (d - t.astype(F32) * m)
            dqkv_ref[rows, cut] = (u * cosine - swap16(u) * sine).astype(BF16)
        for g in groups:
            dqkv_ref[rows, 1024 + 128 * g : 1024 + 128 * g + 128] = dv[g].astype(BF16)

    for w in range(4):
        window(w)

    dn_ref[...] = mt(dqkv_ref[...], wqkv_ref[...])
    total = jnp.zeros((1, 512), F32)
    for w in range(4):
        rows = slice(64 * w, 64 * w + 64)
        xs = x_ref[rows, :].astype(F32)
        inv = lax.rsqrt(jnp.mean(xs * xs, -1, keepdims=True) + 1e-05)
        total = total + jnp.sum(dn_ref[rows, :] * xs * inv, 0, keepdims=True)

    hi, lo = split2(total)
    row16 = iota((16, 128), 0)
    tail = jnp.zeros((16, 128), F32)
    for j in range(4):
        cut = slice(128 * j, 128 * j + 128)
        tail = jnp.where(row16 == j, hi[:, cut].astype(F32), tail)
        tail = jnp.where(row16 == j + 4, lo[:, cut].astype(F32), tail)
    tail = tail.astype(BF16)
    tail_ref[...] = tail

    nt_ref[...] = n_ref[...].T.reshape(16, 2, 16, 256)
    at_ref[...] = att_ref[...].T.reshape(16, 2, 16, 256)
    products(send_ref, 1 - core, xpos, nt_ref, at_ref, dqkv_ref, dy_ref, tail)


def products(out_ref, half, xpos, nt_ref, at_ref, dqkv_ref, dy_ref, tail):
    low64 = iota((256, 128), 1) < 64
    nt = nt_ref[:, half].reshape(256, 256)
    at = at_ref[:, half].reshape(256, 256)
    for p in range(4):
        gq = mm(nt, dqkv_ref[:, 384 * p : 384 * p + 384])
        go = pltpu.roll(mm(at, dy_ref[:, 128 * p : 128 * p + 128]), 64, 1)
        mid = gq[:, 128:256]
        parts = (
            gq[:, 0:128], jnp.where(low64, mid, go),
            gq[:, 256:384], jnp.where(low64, go, mid),
        )
        rel = lax.bitwise_xor(xpos, jnp.int32(p))
        for j, part in enumerate(parts):
            part = part.astype(BF16)
            for i in range(16):
                at_row = 16 + 64 * i + 16 * j
                out_ref[rel, at_row : at_row + 16, :] = part[16 * i : 16 * i + 16, :]
        out_ref[rel, 0:16, :] = tail


def second_kernel(place, dy_ref, dqkv_ref, nt_ref, at_ref, tail_ref, keep_ref):
    products(keep_ref, place[0], place[1], nt_ref, at_ref, dqkv_ref, dy_ref, tail_ref[...])


def branch_kernel(x_ref, dn_ref, gain_ref, diag_ref, above_ref, west_ref, own_ref):
    gain = gain_ref[...]
    for w in range(4):
        rows = slice(64 * w, 64 * w + 64)
        xs = x_ref[rows, :].astype(F32)
        inv = lax.rsqrt(jnp.mean(xs * xs, -1, keepdims=True) + 1e-05)
        scaled = dn_ref[rows, :] * gain
        back = inv * scaled - xs * (inv * inv * inv) * jnp.mean(xs * scaled, -1, keepdims=True)
        back = back.reshape(8, 8, 512)
        diag_ref[w] = back[:4, :4].astype(BF16)
        above_ref[w] = back[:4, 4:].astype(BF16)
        west_ref[w] = back[4:, :4].astype(BF16)
        own_ref[w] = back[4:, 4:].astype(BF16)


def add_tails(tails):
    total = sum(t.astype(F32) for t in tails)
    row = iota((16, 128), 0)
    both = total + pltpu.roll(total, 12, 0)
    hi = both.astype(BF16).astype(F32)
    lo = pltpu.roll(both - hi, 4, 0)
    return jnp.where(row < 4, hi, jnp.where(row < 8, lo, 0.0)).astype(BF16)


def add(*parts):
    return sum(p.astype(F32) for p in parts).astype(BF16)


def pair_kernel(keep_ref, got_ref, a_keep, a_give, b_keep, b_give):
    for k in range(4):
        a_ref = (a_keep if k in (0, 3) else a_give).at[0 if k in (0, 1) else 1]
        b_ref = (b_keep if k in (0, 1) else b_give).at[0 if k in (0, 3) else 1]
        a_ref[0:16] = add_tails([keep_ref[k, 0:16, :], got_ref[k, 0:16, :]])
        a_ref[16:528] = add(keep_ref[k, 16:528, :], got_ref[k, 16:528, :])
        b_ref[...] = add(keep_ref[k, 528:1040, :], got_ref[k, 528:1040, :])


def first_x_kernel(a_ref, a_got, b_ref, b_got, a_mine, a_give, b_mine, b_give):
    for k, (a_out, b_out) in enumerate(((a_mine, b_mine), (a_give, b_give))):
        a_out[0:16] = add_tails([a_ref[k, 0:16], a_got[k, 0:16]])
        a_out[16:528] = add(a_ref[k, 16:528], a_got[k, 16:528])
        b_out[...] = add(b_ref[k], b_got[k])


def second_x_kernel(a_ref, a_got, b_ref, b_got, out_ref):
    out_ref[0:16, 0:32, :] = add(a_ref[16:528, :], a_got[16:528, :]).reshape(16, 32, 128)
    out_ref[16:32, 0:32, :] = add(b_ref[...], b_got[...]).reshape(16, 32, 128)
    tail = add_tails([a_ref[0:16, :], a_got[0:16, :]])
    out_ref[:, 32:40, :] = jnp.broadcast_to(tail[None, 0:8], (32, 8, 128))


def last_kernel(place, in_ref, qkv_ref, out_ref, gain_ref):
    total = jnp.sum(in_ref[...].astype(F32), 0)
    one, two, tail = total[0:16], total[16:32], total[32:40]
    low = iota((16, 128), 1) < 64
    even = place[3] == 0
    one_r, two_r = pltpu.roll(one, 64, 1), pltpu.roll(two, 64, 1)
    qkv_ref[:, 0:128] = jnp.where(even, one, jnp.where(low, two_r, one_r))
    qkv_ref[:, 128:192] = jnp.where(even, two, one_r)[:, 0:64]
    out_ref[...] = jnp.where(even, two_r, two)[:, 0:64]
    gain_ref[...] = tail[0:4] + tail[4:8]


SMEM = pl.BlockSpec(memory_space=pltpu.SMEM)
VMEM = pl.BlockSpec(memory_space=pltpu.VMEM)
PARAMS = pltpu.CompilerParams(vmem_limit_bytes=24 * 1024 * 1024)


def shape(dims, kind=BF16):
    return jax.ShapeDtypeStruct(dims, kind)


def per_device(tokens, cotangent, norm_gain, w_qkv, w_out):
    zi, hi, core = lax.axis_index("z"), lax.axis_index("yh"), lax.axis_index("c")
    xi, lo = lax.axis_index("x"), lax.axis_index("yl")
    lat, lon = xi * 2 + lo, (zi * 2 + hi) * 2 + core
    place = jnp.stack([core, xi, (lat == 7).astype(jnp.int32), lo]).astype(jnp.int32)

    every = ("z", "yh", "c", "x", "yl")

    def send(v, dlon, dlat):
        pairs = [
            (i * 8 + j, (i + dlon) % 32 * 8 + (j + dlat) % 8) for i in range(32) for j in range(8)
        ]
        return lax.ppermute(v, every, pairs)

    diag, east, below, own = pl.pallas_call(
        quads_kernel,
        out_shape=(shape((2, 4, 4, 4, 512)),) * 4,
        in_specs=[pl.BlockSpec(memory_space=pl.ANY)] * 2,
        out_specs=(VMEM,) * 4,
        scratch_shapes=[pltpu.VMEM((2, 4, 8, 8, 512), BF16), pltpu.SemaphoreType.DMA((2, 4))],
        compiler_params=PARAMS,
        name="quads",
    )(*(pltpu.with_memory_space_constraint(v, pltpu.HBM) for v in (tokens, cotangent)))
    diag, east, below = send(diag, -1, -1), send(east, -1, 0), send(below, 0, -1)
    win = jnp.concatenate(
        [jnp.concatenate([diag, below], 3), jnp.concatenate([east, own], 3)], 2
    )
    xw = win[0].reshape(256, 512)
    dyw = win[1].reshape(256, 512)

    cell = jnp.arange(64, dtype=jnp.int32)[:, None]
    entry = jnp.arange(128, dtype=jnp.int32)[None, :]
    r, c = cell // 8, cell % 8
    prow = (lat * 8 + r + jnp.where(r < 4, 8, 0)).astype(F32)
    pcol = (lon * 8 + c + jnp.where(c < 4, 8, 0)).astype(F32)
    freqs = 100.0 ** (-(entry % 8).astype(F32) / 8.0)
    angle = jnp.where(entry % 16 < 8, prow, pcol) * freqs
    cosine = jnp.cos(angle)
    sine = jnp.sin(angle) * jnp.where(entry % HD < 16, -1.0, 1.0)

    gain_row = norm_gain.reshape(1, 512)
    normed, qk, value, scales = pl.pallas_call(
        forward_kernel,
        out_shape=(
            shape((256, 512)), shape((256, 1024)), shape((256, 512)), shape((256, 1024), F32),
        ),
        in_specs=[VMEM] * 5,
        out_specs=(VMEM,) * 4,
        scratch_shapes=[pltpu.VMEM((256, 1536), F32)],
        compiler_params=PARAMS,
        cost_estimate=pl.CostEstimate(flops=400_000_000, bytes_accessed=5_000_000, transcendentals=0),
        name="window_forward",
    )(xw, gain_row, w_qkv, cosine, sine)
    give, dqkv, dn, nt, at, tail = pl.pallas_call(
        backward_kernel,
        out_shape=(
            shape((4, ROWS, 128)), shape((256, 1536)), shape((256, 512), F32),
            shape((16, 2, 16, 256)), shape((16, 2, 16, 256)), shape((16, 128)),
        ),
        in_specs=[SMEM] + [VMEM] * 10,
        out_specs=(VMEM,) * 6,
        scratch_shapes=[pltpu.VMEM((256, 512), BF16)] * 2,
        compiler_params=PARAMS,
        name="window_backward",
    )(place, xw, dyw, w_qkv, w_out, cosine, sine, normed, qk, value, scales)

    got = lax.ppermute(give, "c", [(0, 1), (1, 0)])
    keep = pl.pallas_call(
        second_kernel,
        out_shape=shape((4, ROWS, 128)),
        in_specs=[SMEM] + [VMEM] * 5,
        out_specs=VMEM,
        compiler_params=PARAMS,
        cost_estimate=pl.CostEstimate(flops=300_000_000, bytes_accessed=4_000_000, transcendentals=0),
        name="kept_half",
    )(place, dyw, dqkv, nt, at, tail)
    def along_x(v, mask):
        return lax.ppermute(v, "x", [(i, i ^ mask) for i in range(4)])

    a_keep, a_give, b_keep, b_give = pl.pallas_call(
        pair_kernel,
        out_shape=(shape((2, 528, 128)),) * 2 + (shape((2, 512, 128)),) * 2,
        in_specs=[VMEM] * 2,
        out_specs=(VMEM,) * 4,
        compiler_params=PARAMS,
        name="pair_sum",
    )(keep, got)
    a_give, b_give, dn = lax.optimization_barrier((a_give, b_give, dn))
    a_got, b_got = along_x(a_give, 1), along_x(b_give, 3)
    diag, above, west, own = pl.pallas_call(
        branch_kernel,
        out_shape=(shape((4, 4, 4, 512)),) * 4,
        in_specs=[VMEM] * 3,
        out_specs=(VMEM,) * 4,
        compiler_params=PARAMS,
        cost_estimate=pl.CostEstimate(flops=10_000_000, bytes_accessed=2_000_000, transcendentals=0),
        name="norm_backward",
    )(xw, dn, gain_row)
    top = jnp.concatenate([send(diag, 1, 1), send(above, 0, 1)], 2)
    bottom = jnp.concatenate([send(west, 1, 0), own], 2)
    owned = jnp.concatenate([top, bottom], 1)
    grad_tokens = (cotangent.astype(F32) + owned.astype(F32)).astype(BF16)
    a_mine, a_give, b_mine, b_give = pl.pallas_call(
        first_x_kernel,
        out_shape=(shape((528, 128)),) * 2 + (shape((512, 128)),) * 2,
        in_specs=[VMEM] * 4,
        out_specs=(VMEM,) * 4,
        compiler_params=PARAMS,
        name="first_x_sum",
    )(a_keep, a_got, b_keep, b_got)
    parts = pl.pallas_call(
        second_x_kernel,
        out_shape=shape((32, 40, 128)),
        in_specs=[VMEM] * 4,
        out_specs=VMEM,
        compiler_params=PARAMS,
        name="second_x_sum",
    )(a_mine, along_x(a_give, 3), b_mine, along_x(b_give, 1))
    parts, grad_tokens = lax.optimization_barrier((parts, grad_tokens))
    parts = lax.all_to_all(parts, ("z", "yh", "yl"), 0, 0, tiled=True)
    qkv_share, out_share, gain_share = pl.pallas_call(
        last_kernel,
        out_shape=(shape((16, 192), F32), shape((16, 64), F32), shape((4, 128), F32)),
        in_specs=[SMEM, VMEM],
        out_specs=(VMEM,) * 3,
        compiler_params=PARAMS,
        name="last_sum",
    )(place, parts)
    return (grad_tokens, qkv_share, out_share, gain_share.reshape(512))


def solution(mesh):
    fine = Mesh(mesh.devices.reshape(8, 2, 2, 4, 2), ("z", "yh", "c", "x", "yl"))
    lon, lat = ("z", "yh", "c"), ("x", "yl")
    placed = (P(None, lat, lon, None), P(None, lat, lon, None), P(), P(), P())
    return jax.shard_map(
        per_device,
        mesh=fine,
        in_specs=placed,
        out_specs=(P(None, lat, lon, None), P(lon, lat), P(lon, lat), P()),
        check_vma=False,
    )
```

profile of v0, /device:TPU:6, one launch (start us, length us, event | category | flops | bytes accessed | tf_op | source)
XLA Modules:
  0.0 64.5 jit_solution(14161453994384089465)
XLA Ops:
  0.6 1.1 %quads.1 = (bf16[2,4,4,4,512]{4,3,2,1,0:T(4,128)(2,1)S(1)}, bf16[2,4,4,4,512]{4,3,2,1,0:T(4,128)(2,1)S(1)}, bf16[2,4,4,4,512]{4,3,2,1,0:T(4,128)(2,1)S(1)}, bf16[2,4,4,4,512]{4,3,2,1,0:T(4,128)(2,1)S(1)}) custom-call(bf16[4,8,8,512]{3,2,1,0:T(8,128)(2,1)} %x_ref.1, bf16[4,8,8,512]{3,2,1,0:T(8,128)(2,1)} %dy_ref.1), custom_call_target="tpu_custom_call" | custom-call | tf_op jit(solution)/shard_map/quads/pallas_call | solution.py:284
  1.8 8.1 %collective-permute-start = (bf16[2,4,4,4,512]{4,3,2,1,0:T(4,128)(2,1)S(1)}, bf16[2,4,4,4,512]{4,3,2,1,0:T(4,128)(2,1)S(1)}, u32[]{:S(2)}, u32[]{:S(2)}) collective-permute-start(bf16[2,4,4,4,512]{4,3,2,1,0:T(4,128)(2,1)S(1)} %get-tuple-element.38), channel_id=1, source_target_pairs={{0,255},{1,248},{2,249},{3,250},{4,251},{5,252},{6,253},{7,254},{8... | collective-permute-start | bytes 393224 | tf_op jit(solution)/shard_map/ppermute | solution.py:282
  9.9 0.1 collective-permute-start.1
  10.0 2.1 %collective-permute-start.2 = (bf16[2,4,4,4,512]{4,3,2,1,0:T(4,128)(2,1)S(1)}, bf16[2,4,4,4,512]{4,3,2,1,0:T(4,128)(2,1)S(1)}, u32[]{:S(2)}, u32[]{:S(2)}) collective-permute-start(bf16[2,4,4,4,512]{4,3,2,1,0:T(4,128)(2,1)S(1)} %get-tuple-element.40), channel_id=1, source_target_pairs={{0,248},{1,249},{2,250},{3,251},{4,252},{5,253},{6,254},{7,255},{8... | collective-permute-start | bytes 393224 | tf_op jit(solution)/shard_map/ppermute | solution.py:282
  12.1 0.2 sine_multiply_fusion
  12.3 0.0 copy-start
  12.3 0.0 copy-start.2
  12.4 0.1 pad_add_fusion.place
  12.4 0.0 collective-permute-done
  12.4 2.4 %collective-permute-done.1 = bf16[2,4,4,4,512]{4,3,2,1,0:T(4,128)(2,1)S(1)} collective-permute-done((bf16[2,4,4,4,512]{4,3,2,1,0:T(4,128)(2,1)S(1)}, bf16[2,4,4,4,512]{4,3,2,1,0:T(4,128)(2,1)S(1)}, u32[]{:S(2)}, u32[]{:S(2)}) %collective-permute-start.1) | collective-permute-done | bytes 131104 | tf_op jit(solution)/shard_map/ppermute | solution.py:282
  14.8 0.0 collective-permute-done.2
  14.8 0.3 maximum_maximum_fusion
  15.2 0.0 copy-start.1
  15.2 0.0 copy-done
  15.2 0.0 copy-done.2
  15.2 1.1 %window_forward.1 = (bf16[256,512]{1,0:T(8,128)(2,1)S(1)}, bf16[256,1024]{1,0:T(8,128)(2,1)S(1)}, bf16[256,512]{1,0:T(8,128)(2,1)S(1)}, f32[256,1024]{1,0:T(8,128)S(1)}) custom-call(bf16[256,512]{1,0:T(8,128)(2,1)S(1)} %bitcast.8, f32[1,512]{1,0:T(1,128)S(1)} %bitcast.13, bf16[512,1536]{1,0:T(8,128)(2,1)S(1)} %copy-done, ...), custom_call_target="tpu_custom_call" | custom-call | flops 400000000 | bytes 5000000 | tf_op jit(solution)/shard_map/window_forward/pallas_call | solution.py:311
  16.3 0.0 copy-done.1
  16.3 5.6 %window_backward.1 = (bf16[4,1040,128]{2,1,0:T(8,128)(2,1)S(1)}, bf16[256,1536]{1,0:T(8,128)(2,1)S(1)}, f32[256,512]{1,0:T(8,128)S(1)}, bf16[16,2,16,256]{3,2,1,...) custom-call(s32[4]{0:T(128)S(1)} %pad_add_fusion.place, ...), custom_call_target="tpu_custom_call" | custom-call | tf_op jit(solution)/shard_map/window_backward/pallas_call | solution.py:323
  21.9 0.1 collective-permute-start.3
  22.0 1.2 %kept_half.1.keep_ref = bf16[4,1040,128]{2,1,0:T(8,128)(2,1)S(1)} custom-call(s32[4]{0:T(128)S(1)} %pad_add_fusion.place, bf16[256,512]{1,0:T(8,128)(2,1)S(1)} %bitcast.12, bf16[256,1536]{1,0:T(8,128)(2,1)S(1)} %get-tuple-element.46.dqkv_ref, bf16[16,2,16,256]{3,2,1,0:T(8,128)(2,1)S(1)} %get-tuple-element.47.nt_ref, ...), custom_call_target="tpu_custom_call" | custom-call | flops 300000000 | bytes 4000000 | tf_op jit(solution)/shard_map/kept_half/pallas_call | solution.py:337
  23.2 1.5 %collective-permute-done.3.got_ref = bf16[4,1040,128]{2,1,0:T(8,128)(2,1)S(1)} collective-permute-done((bf16[4,1040,128]{2,1,0:T(8,128)(2,1)S(1)}, bf16[4,1040,128]{2,1,0:T(8,128)(2,1)S(1)}, u32[]{:S(2)}, u32[]{:S(2)}) %collective-permute-start.3) | collective-permute-done | bytes 1064992 | tf_op jit(solution)/shard_map/ppermute | solution.py:336
  24.7 0.3 pair_sum.1
  25.0 0.0 copy-start.3
  25.0 0.6 collective-permute-start.4
  25.6 2.0 %collective-permute-start.5 = (bf16[2,512,128]{2,1,0:T(8,128)(2,1)S(1)}, bf16[2,512,128]{2,1,0:T(8,128)(2,1)S(1)}, u32[]{:S(2)}, u32[]{:S(2)}) collective-permute-start(bf16[2,512,128]{2,1,0:T(8,128)(2,1)S(1)} %get-tuple-element.57), channel_id=1, source_target_pairs={{0,6},{2,4},{4,2},{6,0},{1,7},{3,5},{5,3},{7,1},{8,14},{10,12},{12... | collective-permute-start | bytes 786440 | tf_op jit(solution)/shard_map/ppermute | solution.py:347
  27.6 0.2 norm_backward.1
  27.8 0.1 collective-permute-start.8
  27.9 1.9 %collective-permute-start.9 = (bf16[4,4,4,512]{3,2,1,0:T(4,128)(2,1)S(1)}, bf16[4,4,4,512]{3,2,1,0:T(4,128)(2,1)S(1)}, u32[]{:S(2)}, u32[]{:S(2)}) collective-permute-start(bf16[4,4,4,512]{3,2,1,0:T(4,128)(2,1)S(1)} %get-tuple-element.64), channel_id=1, source_target_pairs={{0,1},{1,2},{2,3},{3,4},{4,5},{5,6},{6,7},{7,0},{8,9},{9,10},{10,1... | collective-permute-start | bytes 196616 | tf_op jit(solution)/shard_map/ppermute | solution.py:282
  29.8 0.0 collective-permute-start.10
  29.8 5.1 %collective-permute-done.5.b_got = bf16[2,512,128]{2,1,0:T(8,128)(2,1)S(1)} collective-permute-done((bf16[2,512,128]{2,1,0:T(8,128)(2,1)S(1)}, bf16[2,512,128]{2,1,0:T(8,128)(2,1)S(1)}, u32[]{:S(2)}, u32[]{:S(2)}) %collective-permute-start.5) | collective-permute-done | bytes 262176 | tf_op jit(solution)/shard_map/ppermute | solution.py:347
  34.9 0.0 collective-permute-done.4.a_got
  34.9 0.1 first_x_sum.1
  35.0 0.4 collective-permute-start.7
  35.4 2.3 %collective-permute-start.6 = (bf16[528,128]{1,0:T(8,128)(2,1)S(1)}, bf16[528,128]{1,0:T(8,128)(2,1)S(1)}, u32[]{:S(2)}, u32[]{:S(2)}) collective-permute-start(bf16[528,128]{1,0:T(8,128)(2,1)S(1)} %get-tuple-element.59), channel_id=1, source_target_pairs={{0,6},{2,4},{4,2},{6,0},{1,7},{3,5},{5,3},{7,1},{8,14},{10,12},{12... | collective-permute-start | bytes 405512 | tf_op jit(solution)/shard_map/ppermute | solution.py:347
  37.8 0.0 collective-permute-done.8
  37.8 0.0 collective-permute-done.9
  37.8 0.0 collective-permute-done.10
  37.8 0.0 copy-done.3
  37.8 0.9 %add_convert_fusion = bf16[4,8,8,512]{3,2,1,0:T(8,128)(2,1)} fusion(bf16[4,8,8,512]{3,2,1,0:T(8,128)(2,1)S(1)} %copy-done.3, bf16[4,4,4,512]{3,2,1,0:T(4,128)(2,1)S(1)} %get-tuple-element.66, bf16[4,4,4,512]{3,2,1,0:T(4,128)(2,1)S(1)} %collective-permute-done.10, bf16[4,4,4,512]{3,2,1,0:T(4,128)(2,1)S(1)} %collective-permute-done.9, ...), kind=kLoop, calls=%fused_computation.1 | loop fusion | flops 1441792 | bytes 786432 | tf_op jit(solution)/shard_map/convert_element_type | solution.py:371
  38.7 1.4 %collective-permute-done.7.b_got = bf16[512,128]{1,0:T(8,128)(2,1)S(1)} collective-permute-done((bf16[512,128]{1,0:T(8,128)(2,1)S(1)}, bf16[512,128]{1,0:T(8,128)(2,1)S(1)}, u32[]{:S(2)}, u32[]{:S(2)}) %collective-permute-start.7) | collective-permute-done | bytes 131104 | tf_op jit(solution)/shard_map/ppermute | solution.py:347
  40.1 1.6 %collective-permute-done.6.a_got = bf16[528,128]{1,0:T(8,128)(2,1)S(1)} collective-permute-done((bf16[528,128]{1,0:T(8,128)(2,1)S(1)}, bf16[528,128]{1,0:T(8,128)(2,1)S(1)}, u32[]{:S(2)}, u32[]{:S(2)}) %collective-permute-start.6) | collective-permute-done | bytes 135200 | tf_op jit(solution)/shard_map/ppermute | solution.py:347
  41.7 0.1 second_x_sum.1
  41.8 21.5 %all_to_all.5.in_ref = bf16[32,40,128]{2,1,0:T(8,128)(2,1)S(1)} all-to-all(bf16[32,40,128]{2,1,0:T(8,128)(2,1)S(1)} %second_x_sum.1), channel_id=1, replica_groups=mesh['z'=8,'yh'=2,'c'=2,'x'=4,'yl'=2] {'z','yh','yl'}, dimensions={0} | all-to-all | bytes 655360 | tf_op jit(solution)/shard_map/all_to_all | solution.py:389
  63.2 1.3 %last_sum.1 = (f32[16,192]{1,0:T(8,128)}, f32[16,64]{1,0:T(8,128)}, f32[4,128]{1,0:T(4,128)}) custom-call(s32[4]{0:T(128)S(1)} %pad_add_fusion.place, bf16[32,40,128]{2,1,0:T(8,128)(2,1)S(1)} %all_to_all.5.in_ref), custom_call_target="tpu_custom_call" | custom-call | tf_op jit(solution)/shard_map/last_sum/pallas_call | solution.py:390
  (4 shorter events, 0.1 us)
Async XLA Ops:
  1.8 10.7 %collective-permute-start = (bf16[2,4,4,4,512]{4,3,2,1,0:T(4,128)(2,1)S(1)}, bf16[2,4,4,4,512]{4,3,2,1,0:T(4,128)(2,1)S(1)}, u32[]{:S(2)}, u32[]{:S(2)}) collective-permute-start(bf16[2,4,4,4,512]{4,3,2,1,0:T(4,128)(2,1)S(1)} %get-tuple-element.38), channel_id=1, source_target_pairs={{0,255},{1,248},{2,249},{3,250},{4,251},{5,252},{6,253},{7,254},{8... | collective-permute-start | bytes 393224 | tf_op jit(solution)/shard_map/ppermute | solution.py:282
  9.9 5.0 %collective-permute-start.1 = (bf16[2,4,4,4,512]{4,3,2,1,0:T(4,128)(2,1)S(1)}, bf16[2,4,4,4,512]{4,3,2,1,0:T(4,128)(2,1)S(1)}, u32[]{:S(2)}, u32[]{:S(2)}) collective-permute-start(bf16[2,4,4,4,512]{4,3,2,1,0:T(4,128)(2,1)S(1)} %get-tuple-element.39), channel_id=1, source_target_pairs={{0,7},{1,0},{2,1},{3,2},{4,3},{5,4},{6,5},{7,6},{8,15},{9,8},{10,9... | collective-permute-start | bytes 393224 | tf_op jit(solution)/shard_map/ppermute | solution.py:282
  10.0 4.8 %collective-permute-start.2 = (bf16[2,4,4,4,512]{4,3,2,1,0:T(4,128)(2,1)S(1)}, bf16[2,4,4,4,512]{4,3,2,1,0:T(4,128)(2,1)S(1)}, u32[]{:S(2)}, u32[]{:S(2)}) collective-permute-start(bf16[2,4,4,4,512]{4,3,2,1,0:T(4,128)(2,1)S(1)} %get-tuple-element.40), channel_id=1, source_target_pairs={{0,248},{1,249},{2,250},{3,251},{4,252},{5,253},{6,254},{7,255},{8... | collective-permute-start | bytes 393224 | tf_op jit(solution)/shard_map/ppermute | solution.py:282
  12.3 2.9 %copy-start = (bf16[512,1536]{1,0:T(8,128)(2,1)S(1)}, bf16[512,1536]{1,0:T(8,128)(2,1)}, u32[]{:S(2)}) copy-start(bf16[512,1536]{1,0:T(8,128)(2,1)} %wqkv_ref.3) | copy-start | bytes 4718596
  12.3 2.9 %copy-start.2 = (f32[512]{0:T(512)S(1)}, f32[512]{0:T(512)}, u32[]{:S(2)}) copy-start(f32[512]{0:T(512)} %param.7) | copy-start | bytes 6148
  15.2 1.2 %copy-start.1 = (bf16[512,512]{1,0:T(8,128)(2,1)S(1)}, bf16[512,512]{1,0:T(8,128)(2,1)}, u32[]{:S(2)}) copy-start(bf16[512,512]{1,0:T(8,128)(2,1)} %wout_ref.1) | copy-start | bytes 1572868
  21.9 2.8 %collective-permute-start.3 = (bf16[4,1040,128]{2,1,0:T(8,128)(2,1)S(1)}, bf16[4,1040,128]{2,1,0:T(8,128)(2,1)S(1)}, u32[]{:S(2)}, u32[]{:S(2)}) collective-permute-start(bf16[4,1040,128]{2,1,0:T(8,128)(2,1)S(1)} %get-tuple-element.50), channel_id=1, source_target_pairs={{0,8},{8,0},{1,9},{9,1},{2,10},{10,2},{3,11},{11,3},{4,12},{12,4},... | collective-permute-start | bytes 3194888 | tf_op jit(solution)/shard_map/ppermute | solution.py:336
  25.0 12.9 %copy-start.3 = (bf16[4,8,8,512]{3,2,1,0:T(8,128)(2,1)S(1)}, bf16[4,8,8,512]{3,2,1,0:T(8,128)(2,1)}, u32[]{:S(2)}) copy-start(bf16[4,8,8,512]{3,2,1,0:T(8,128)(2,1)} %dy_ref.1) | copy-start | bytes 786436
  25.0 9.9 %collective-permute-start.4 = (bf16[2,528,128]{2,1,0:T(8,128)(2,1)S(1)}, bf16[2,528,128]{2,1,0:T(8,128)(2,1)S(1)}, u32[]{:S(2)}, u32[]{:S(2)}) collective-permute-start(bf16[2,528,128]{2,1,0:T(8,128)(2,1)S(1)} %get-tuple-element.55), channel_id=1, source_target_pairs={{0,2},{2,0},{4,6},{6,4},{1,3},{3,1},{5,7},{7,5},{8,10},{10,8},{12,... | collective-permute-start | bytes 811016 | tf_op jit(solution)/shard_map/ppermute | solution.py:347
  25.6 9.3 %collective-permute-start.5 = (bf16[2,512,128]{2,1,0:T(8,128)(2,1)S(1)}, bf16[2,512,128]{2,1,0:T(8,128)(2,1)S(1)}, u32[]{:S(2)}, u32[]{:S(2)}) collective-permute-start(bf16[2,512,128]{2,1,0:T(8,128)(2,1)S(1)} %get-tuple-element.57), channel_id=1, source_target_pairs={{0,6},{2,4},{4,2},{6,0},{1,7},{3,5},{5,3},{7,1},{8,14},{10,12},{12... | collective-permute-start | bytes 786440 | tf_op jit(solution)/shard_map/ppermute | solution.py:347
  27.8 10.0 %collective-permute-start.8 = (bf16[4,4,4,512]{3,2,1,0:T(4,128)(2,1)S(1)}, bf16[4,4,4,512]{3,2,1,0:T(4,128)(2,1)S(1)}, u32[]{:S(2)}, u32[]{:S(2)}) collective-permute-start(bf16[4,4,4,512]{3,2,1,0:T(4,128)(2,1)S(1)} %get-tuple-element.63), channel_id=1, source_target_pairs={{0,9},{1,10},{2,11},{3,12},{4,13},{5,14},{6,15},{7,8},{8,17},{9,18... | collective-permute-start | bytes 196616 | tf_op jit(solution)/shard_map/ppermute | solution.py:282
  27.9 9.9 %collective-permute-start.9 = (bf16[4,4,4,512]{3,2,1,0:T(4,128)(2,1)S(1)}, bf16[4,4,4,512]{3,2,1,0:T(4,128)(2,1)S(1)}, u32[]{:S(2)}, u32[]{:S(2)}) collective-permute-start(bf16[4,4,4,512]{3,2,1,0:T(4,128)(2,1)S(1)} %get-tuple-element.64), channel_id=1, source_target_pairs={{0,1},{1,2},{2,3},{3,4},{4,5},{5,6},{6,7},{7,0},{8,9},{9,10},{10,1... | collective-permute-start | bytes 196616 | tf_op jit(solution)/shard_map/ppermute | solution.py:282
  29.8 8.0 %collective-permute-start.10 = (bf16[4,4,4,512]{3,2,1,0:T(4,128)(2,1)S(1)}, bf16[4,4,4,512]{3,2,1,0:T(4,128)(2,1)S(1)}, u32[]{:S(2)}, u32[]{:S(2)}) collective-permute-start(bf16[4,4,4,512]{3,2,1,0:T(4,128)(2,1)S(1)} %get-tuple-element.65), channel_id=1, source_target_pairs={{0,8},{1,9},{2,10},{3,11},{4,12},{5,13},{6,14},{7,15},{8,16},{9,17... | collective-permute-start | bytes 196616 | tf_op jit(solution)/shard_map/ppermute | solution.py:282
  35.0 5.1 %collective-permute-start.7 = (bf16[512,128]{1,0:T(8,128)(2,1)S(1)}, bf16[512,128]{1,0:T(8,128)(2,1)S(1)}, u32[]{:S(2)}, u32[]{:S(2)}) collective-permute-start(bf16[512,128]{1,0:T(8,128)(2,1)S(1)} %get-tuple-element.61), channel_id=1, source_target_pairs={{0,2},{2,0},{4,6},{6,4},{1,3},{3,1},{5,7},{7,5},{8,10},{10,8},{12,... | collective-permute-start | bytes 393224 | tf_op jit(solution)/shard_map/ppermute | solution.py:347
  35.4 6.2 %collective-permute-start.6 = (bf16[528,128]{1,0:T(8,128)(2,1)S(1)}, bf16[528,128]{1,0:T(8,128)(2,1)S(1)}, u32[]{:S(2)}, u32[]{:S(2)}) collective-permute-start(bf16[528,128]{1,0:T(8,128)(2,1)S(1)} %get-tuple-element.59), channel_id=1, source_target_pairs={{0,6},{2,4},{4,2},{6,0},{1,7},{3,5},{5,3},{7,1},{8,14},{10,12},{12... | collective-permute-start | bytes 405512 | tf_op jit(solution)/shard_map/ppermute | solution.py:347
where the time goes:
time: 64.7 us; the launch traced here: 64.5 us
  blocking collectives  21.5 us (33%)
  starting transfers between devices  17.7 us (27%)
  waiting for transfers between devices  11.9 us (18%)
  Pallas kernels  11.1 us (17%)
  other arithmetic  1.44 us (2%)
  between operations  0.8 us (1%)
    all_to_all x1, blocking collectives, per_device(): parts = lax.all_to_all(parts, ('z', 'yh', 'yl'), 0, 0, tiled=True)  21.5 us
    ppermute x6, starting transfers between devices, send(): return lax.ppermute(v, every, pairs)  12.3 us
    ppermute x4, waiting for transfers between devices, along_x(): return lax.ppermute(v, 'x', [(i, i ^ mask) for i in range(4)])  8.04 us
    pallas_call x1, Pallas kernels, per_device(): pl.pallas_call(backward_kernel, out_shape=(shape((4, ROWS, 128)), shape((...  5.59 us
    ppermute x4, starting transfers between devices, along_x(): return lax.ppermute(v, 'x', [(i, i ^ mask) for i in range(4)])  5.37 us
    ppermute x6, waiting for transfers between devices, send(): return lax.ppermute(v, every, pairs)  2.42 us
    ppermute x1, waiting for transfers between devices, per_device(): got = lax.ppermute(give, 'c', [(0, 1), (1, 0)])  1.46 us
  transfers between devices with their start and end apart: 11, of which 5 were waited for; matrix products, arithmetic and copies ran while one was open for 2% of the time, Pallas kernels for 2%

commit v1 on v0

--- a/solution.py
+++ b/solution.py
@@ -101,51 +101,50 @@
     half_b = iota((64, 256), 1) % 64 // 32
     allowed = jnp.logical_or(half_a == half_b, capped == 0)
     cosine, sine = cos_ref[...], sin_ref[...]
-    groups = range(4)
-
-    def window(w):
-        rows = slice(64 * w, 64 * w + 64)
-        q = [qk_ref[rows, 128 * g : 128 * g + 128] for g in groups]
-        k = [qk_ref[rows, 512 + 128 * g : 512 + 128 * g + 128] for g in groups]
-        v = [v_ref[rows, 128 * g : 128 * g + 128] for g in groups]
-        da = [da_ref[rows, 128 * g : 128 * g + 128] for g in groups]
+    def windows(which):
+        units = [(slice(64 * w, 64 * w + 64), 128 * g) for w in which for g in range(4)]
+        n = range(len(units))
+        q = [qk_ref[rows, c : c + 128] for rows, c in units]
+        k = [qk_ref[rows, 512 + c : 640 + c] for rows, c in units]
+        v = [v_ref[rows, c : c + 128] for rows, c in units]
+        da = [da_ref[rows, c : c + 128] for rows, c in units]
         qb = [spread(t) for t in q]
         kb = [spread(t) for t in k]
         vb = [spread(t) for t in v]
         db = [spread(t) for t in da]
 
-        e = [jnp.where(allowed, jnp.exp2(mt(q[g], kb[g])), 0.0) for g in groups]
-        nd = [mm(e[g].astype(BF16), jnp.concatenate([vb[g], ones_num], axis=1)) for g in groups]
+        e = [jnp.where(allowed, jnp.exp2(mt(q[g], kb[g])), 0.0) for g in n]
+        et = [jnp.where(allowed, jnp.exp2(mt(k[g], qb[g])), 0.0) for g in n]
+        nd = [mm(e[g].astype(BF16), jnp.concatenate([vb[g], ones_num], axis=1)) for g in n]
+        dp = [mt(da[g], vb[g]) for g in n]
+        dpt = [mt(v[g], db[g]) for g in n]
+        pt = [t * (1.0 / jnp.sum(t, 0, keepdims=True)) for t in et]
+        dv = [mm(pt[g].astype(BF16), db[g]) for g in n]
         rden = [1.0 / t[:, 128:] for t in nd]
         att = [t[:, :128] * r for t, r in zip(nd, rden)]
-        for g in groups:
-            att_ref[rows, 128 * g : 128 * g + 128] = att[g].astype(BF16)
-        dp = [mt(da[g], vb[g]) for g in groups]
-        dots = [jnp.concatenate(split2(da[g].astype(F32) * att[g]), axis=1) for g in groups]
+        for g, (rows, c) in enumerate(units):
+            att_ref[rows, c : c + 128] = att[g].astype(BF16)
+            dqkv_ref[rows, 1024 + c : 1152 + c] = dv[g].astype(BF16)
+        dots = [jnp.concatenate(split2(da[g].astype(F32) * att[g]), axis=1) for g in n]
         r = mm(jnp.concatenate(dots, 0), ones_row)
-        xe = [(e[g] * (dp[g] - r[64 * g : 64 * g + 64])).astype(BF16) for g in groups]
-        dqr = [mm(xe[g], kb[g]) * (rden[g] * HD ** (-0.5)) for g in groups]
-        et = [jnp.where(allowed, jnp.exp2(mt(k[g], qb[g])), 0.0) for g in groups]
-        pt = [t * (1.0 / jnp.sum(t, 0, keepdims=True)) for t in et]
-        dpt = [mt(v[g], db[g]) for g in groups]
-        rt = [jnp.sum(pt[g] * dpt[g], 0, keepdims=True) for g in groups]
-        dst = [(pt[g] * (dpt[g] - rt[g])).astype(BF16) for g in groups]
-        dv = [mm(pt[g].astype(BF16), db[g]) for g in groups]
-        dkr = [mm(dst[g], qb[g]) * (1.0 / LOG2E) for g in groups]
-
+        rt = [jnp.sum(pt[g] * dpt[g], 0, keepdims=True) for g in n]
+        dst = [(pt[g] * (dpt[g] - rt[g])).astype(BF16) for g in n]
+        dkr = [mm(dst[g], qb[g]) * (1.0 / LOG2E) for g in n]
+        xe = [(e[g] * (dp[g] - r[64 * g : 64 * g + 64])).astype(BF16) for g in n]
+        dqr = [mm(xe[g], kb[g]) * (rden[g] * HD ** (-0.5)) for g in n]
+
+        places = units + [(rows, 512 + c) for rows, c in units]
         grads, tiles = dqr + dkr, q + k
         dots = [(d * t.astype(F32)).astype(BF16) for d, t in zip(grads, tiles)]
         means = mm(jnp.concatenate(dots, 0), ones32)
         for j, (d, t) in enumerate(zip(grads, tiles)):
-            cut = slice(128 * j, 128 * j + 128)
-            m = means[64 * j : 64 * j + 64] * (1.0 / (HD * QFOLD * QFOLD) if j < 4 else 1.0 / HD)
-            u = scale_ref[rows, cut] * (d - t.astype(F32) * m)
-            dqkv_ref[rows, cut] = (u * cosine - swap16(u) * sine).astype(BF16)
-        for g in groups:
-            dqkv_ref[rows, 1024 + 128 * g : 1024 + 128 * g + 128] = dv[g].astype(BF16)
-
-    for w in range(4):
-        window(w)
+            rows, c = places[j]
+            m = means[64 * j : 64 * j + 64] * (1.0 / (HD * QFOLD * QFOLD) if c < 512 else 1.0 / HD)
+            u = scale_ref[rows, c : c + 128] * (d - t.astype(F32) * m)
+            dqkv_ref[rows, c : c + 128] = (u * cosine - swap16(u) * sine).astype(BF16)
+
+    windows((0, 1))
+    windows((2, 3))
 
     dn_ref[...] = mt(dqkv_ref[...], wqkv_ref[...])
     total = jnp.zeros((1, 512), F32)
@@ -240,22 +239,24 @@
 
 
 def second_x_kernel(a_ref, a_got, b_ref, b_got, out_ref):
-    out_ref[0:16, 0:32, :] = add(a_ref[16:528, :], a_got[16:528, :]).reshape(16, 32, 128)
-    out_ref[16:32, 0:32, :] = add(b_ref[...], b_got[...]).reshape(16, 32, 128)
-    tail = add_tails([a_ref[0:16, :], a_got[0:16, :]])
-    out_ref[:, 32:40, :] = jnp.broadcast_to(tail[None, 0:8], (32, 8, 128))
+    for h, (one, two) in enumerate(((a_ref[16:528, :], a_got[16:528, :]), (b_ref[...], b_got[...]))):
+        total = one.astype(F32) + two.astype(F32)
+        out_ref[16 * h : 16 * h + 16, 0:8] = total.reshape(16, 8, 4, 128).astype(BF16)
+    tail = a_ref[0:16, :].astype(F32) + a_got[0:16, :].astype(F32)
+    tail = (tail[0:4] + tail[4:8]).astype(BF16)
+    out_ref[:, 8] = jnp.broadcast_to(tail[None], (32, 4, 128))
 
 
 def last_kernel(place, in_ref, qkv_ref, out_ref, gain_ref):
     total = jnp.sum(in_ref[...].astype(F32), 0)
-    one, two, tail = total[0:16], total[16:32], total[32:40]
+    one, two, tail = total[0:4].reshape(16, 128), total[4:8].reshape(16, 128), total[8]
     low = iota((16, 128), 1) < 64
     even = place[3] == 0
     one_r, two_r = pltpu.roll(one, 64, 1), pltpu.roll(two, 64, 1)
     qkv_ref[:, 0:128] = jnp.where(even, one, jnp.where(low, two_r, one_r))
     qkv_ref[:, 128:192] = jnp.where(even, two, one_r)[:, 0:64]
     out_ref[...] = jnp.where(even, two_r, two)[:, 0:64]
-    gain_ref[...] = tail[0:4] + tail[4:8]
+    gain_ref[...] = tail
 
 
 SMEM = pl.BlockSpec(memory_space=pltpu.SMEM)
@@ -379,7 +380,7 @@
     )(a_keep, a_got, b_keep, b_got)
     parts = pl.pallas_call(
         second_x_kernel,
-        out_shape=shape((32, 40, 128)),
+        out_shape=shape((32, 9, 4, 128)),
         in_specs=[VMEM] * 4,
         out_specs=VMEM,
         compiler_params=PARAMS,

time: 64.7 us -> 63.7 us (0.985)
    pallas_call x1, Pallas kernels: 5.59 us -> 4.94 us  [per_device(): pl.pallas_call(backward_kernel, out_shape=(shape((4, ROWS, 128)), shape((...]
  transfers between devices with their start and end apart: 11 -> 11, of which waited for: 5 -> 5; matrix products, arithmetic and copies ran while one was open for 2% -> 2% of each run, Pallas kernels for 2% -> 3%
where the time goes in v1:
time: 63.7 us; the launch traced here: 63.5 us
  blocking collectives  21 us (33%)
  starting transfers between devices  17.7 us (28%)
  waiting for transfers between devices  11.9 us (19%)
  Pallas kernels  10.5 us (16%)
  other arithmetic  1.44 us (2%)
  between operations  0.79 us (1%)
    all_to_all x1, blocking collectives, per_device(): parts = lax.all_to_all(parts, ('z', 'yh', 'yl'), 0, 0, tiled=True)  21 us
    ppermute x6, starting transfers between devices, send(): return lax.ppermute(v, every, pairs)  12.3 us
    ppermute x4, waiting for transfers between devices, along_x(): return lax.ppermute(v, 'x', [(i, i ^ mask) for i in range(4)])  8.05 us
    ppermute x4, starting transfers between devices, along_x(): return lax.ppermute(v, 'x', [(i, i ^ mask) for i in range(4)])  5.36 us
    pallas_call x1, Pallas kernels, per_device(): pl.pallas_call(backward_kernel, out_shape=(shape((4, ROWS, 128)), shape((...  4.94 us
    ppermute x6, waiting for transfers between devices, send(): return lax.ppermute(v, every, pairs)  2.42 us
    ppermute x1, waiting for transfers between devices, per_device(): got = lax.ppermute(give, 'c', [(0, 1), (1, 0)])  1.46 us
    pallas_call x1, Pallas kernels, per_device(): pl.pallas_call(last_kernel, out_shape=(shape((16, 192), F32), shape((16,...  1.33 us
  transfers between devices with their start and end apart: 11, of which 5 were waited for; matrix products, arithmetic and copies ran while one was open for 2% of the time, Pallas kernels for 3%

profile of v1, /device:TPU:6, one launch (start us, length us, event | category | flops | bytes accessed | tf_op | source)
XLA Modules:
  0.0 63.5 jit_solution(2175942454305785058)
XLA Ops:
  0.6 1.1 %quads.1 = (bf16[2,4,4,4,512]{4,3,2,1,0:T(4,128)(2,1)S(1)}, bf16[2,4,4,4,512]{4,3,2,1,0:T(4,128)(2,1)S(1)}, bf16[2,4,4,4,512]{4,3,2,1,0:T(4,128)(2,1)S(1)}, bf16[2,4,4,4,512]{4,3,2,1,0:T(4,128)(2,1)S(1)}) custom-call(bf16[4,8,8,512]{3,2,1,0:T(8,128)(2,1)} %x_ref.1, bf16[4,8,8,512]{3,2,1,0:T(8,128)(2,1)} %dy_ref.1), custom_call_target="tpu_custom_call" | custom-call | tf_op jit(solution)/shard_map/quads/pallas_call | solution.py:285
  1.8 8.1 %collective-permute-start = (bf16[2,4,4,4,512]{4,3,2,1,0:T(4,128)(2,1)S(1)}, bf16[2,4,4,4,512]{4,3,2,1,0:T(4,128)(2,1)S(1)}, u32[]{:S(2)}, u32[]{:S(2)}) collective-permute-start(bf16[2,4,4,4,512]{4,3,2,1,0:T(4,128)(2,1)S(1)} %get-tuple-element.38), channel_id=1, source_target_pairs={{0,255},{1,248},{2,249},{3,250},{4,251},{5,252},{6,253},{7,254},{8... | collective-permute-start | bytes 393224 | tf_op jit(solution)/shard_map/ppermute | solution.py:283
  9.9 0.1 collective-permute-start.1
  10.0 2.1 %collective-permute-start.2 = (bf16[2,4,4,4,512]{4,3,2,1,0:T(4,128)(2,1)S(1)}, bf16[2,4,4,4,512]{4,3,2,1,0:T(4,128)(2,1)S(1)}, u32[]{:S(2)}, u32[]{:S(2)}) collective-permute-start(bf16[2,4,4,4,512]{4,3,2,1,0:T(4,128)(2,1)S(1)} %get-tuple-element.40), channel_id=1, source_target_pairs={{0,248},{1,249},{2,250},{3,251},{4,252},{5,253},{6,254},{7,255},{8... | collective-permute-start | bytes 393224 | tf_op jit(solution)/shard_map/ppermute | solution.py:283
  12.1 0.2 sine_multiply_fusion
  12.3 0.0 copy-start
  12.3 0.0 copy-start.2
  12.4 0.1 pad_add_fusion.place
  12.4 0.0 collective-permute-done
  12.4 2.4 %collective-permute-done.1 = bf16[2,4,4,4,512]{4,3,2,1,0:T(4,128)(2,1)S(1)} collective-permute-done((bf16[2,4,4,4,512]{4,3,2,1,0:T(4,128)(2,1)S(1)}, bf16[2,4,4,4,512]{4,3,2,1,0:T(4,128)(2,1)S(1)}, u32[]{:S(2)}, u32[]{:S(2)}) %collective-permute-start.1) | collective-permute-done | bytes 131104 | tf_op jit(solution)/shard_map/ppermute | solution.py:283
  14.8 0.0 collective-permute-done.2
  14.8 0.3 maximum_maximum_fusion
  15.2 0.0 copy-start.1
  15.2 0.0 copy-done
  15.2 0.0 copy-done.2
  15.2 1.1 %window_forward.1 = (bf16[256,512]{1,0:T(8,128)(2,1)S(1)}, bf16[256,1024]{1,0:T(8,128)(2,1)S(1)}, bf16[256,512]{1,0:T(8,128)(2,1)S(1)}, f32[256,1024]{1,0:T(8,128)S(1)}) custom-call(bf16[256,512]{1,0:T(8,128)(2,1)S(1)} %bitcast.8, f32[1,512]{1,0:T(1,128)S(1)} %bitcast.13, bf16[512,1536]{1,0:T(8,128)(2,1)S(1)} %copy-done, ...), custom_call_target="tpu_custom_call" | custom-call | flops 400000000 | bytes 5000000 | tf_op jit(solution)/shard_map/window_forward/pallas_call | solution.py:312
  16.3 0.0 copy-done.1
  16.3 4.9 %window_backward.1 = (bf16[4,1040,128]{2,1,0:T(8,128)(2,1)S(1)}, bf16[256,1536]{1,0:T(8,128)(2,1)S(1)}, f32[256,512]{1,0:T(8,128)S(1)}, bf16[16,2,16,256]{3,2,1,...) custom-call(s32[4]{0:T(128)S(1)} %pad_add_fusion.place, ...), custom_call_target="tpu_custom_call" | custom-call | tf_op jit(solution)/shard_map/window_backward/pallas_call | solution.py:324
  21.3 0.1 collective-permute-start.3
  21.4 1.2 %kept_half.1.keep_ref = bf16[4,1040,128]{2,1,0:T(8,128)(2,1)S(1)} custom-call(s32[4]{0:T(128)S(1)} %pad_add_fusion.place, bf16[256,512]{1,0:T(8,128)(2,1)S(1)} %bitcast.12, bf16[256,1536]{1,0:T(8,128)(2,1)S(1)} %get-tuple-element.46.dqkv_ref, bf16[16,2,16,256]{3,2,1,0:T(8,128)(2,1)S(1)} %get-tuple-element.47.nt_ref, ...), custom_call_target="tpu_custom_call" | custom-call | flops 300000000 | bytes 4000000 | tf_op jit(solution)/shard_map/kept_half/pallas_call | solution.py:338
  22.6 1.5 %collective-permute-done.3.got_ref = bf16[4,1040,128]{2,1,0:T(8,128)(2,1)S(1)} collective-permute-done((bf16[4,1040,128]{2,1,0:T(8,128)(2,1)S(1)}, bf16[4,1040,128]{2,1,0:T(8,128)(2,1)S(1)}, u32[]{:S(2)}, u32[]{:S(2)}) %collective-permute-start.3) | collective-permute-done | bytes 1064992 | tf_op jit(solution)/shard_map/ppermute | solution.py:337
  24.1 0.3 pair_sum.1
  24.3 0.0 copy-start.3
  24.3 0.6 collective-permute-start.4
  24.9 2.0 %collective-permute-start.5 = (bf16[2,512,128]{2,1,0:T(8,128)(2,1)S(1)}, bf16[2,512,128]{2,1,0:T(8,128)(2,1)S(1)}, u32[]{:S(2)}, u32[]{:S(2)}) collective-permute-start(bf16[2,512,128]{2,1,0:T(8,128)(2,1)S(1)} %get-tuple-element.57), channel_id=1, source_target_pairs={{0,6},{2,4},{4,2},{6,0},{1,7},{3,5},{5,3},{7,1},{8,14},{10,12},{12... | collective-permute-start | bytes 786440 | tf_op jit(solution)/shard_map/ppermute | solution.py:348
  26.9 0.2 norm_backward.1
  27.2 0.1 collective-permute-start.8
  27.3 1.9 %collective-permute-start.9 = (bf16[4,4,4,512]{3,2,1,0:T(4,128)(2,1)S(1)}, bf16[4,4,4,512]{3,2,1,0:T(4,128)(2,1)S(1)}, u32[]{:S(2)}, u32[]{:S(2)}) collective-permute-start(bf16[4,4,4,512]{3,2,1,0:T(4,128)(2,1)S(1)} %get-tuple-element.64), channel_id=1, source_target_pairs={{0,1},{1,2},{2,3},{3,4},{4,5},{5,6},{6,7},{7,0},{8,9},{9,10},{10,1... | collective-permute-start | bytes 196616 | tf_op jit(solution)/shard_map/ppermute | solution.py:283
  29.2 0.0 collective-permute-start.10
  29.2 5.1 %collective-permute-done.5.b_got = bf16[2,512,128]{2,1,0:T(8,128)(2,1)S(1)} collective-permute-done((bf16[2,512,128]{2,1,0:T(8,128)(2,1)S(1)}, bf16[2,512,128]{2,1,0:T(8,128)(2,1)S(1)}, u32[]{:S(2)}, u32[]{:S(2)}) %collective-permute-start.5) | collective-permute-done | bytes 262176 | tf_op jit(solution)/shard_map/ppermute | solution.py:348
  34.2 0.0 collective-permute-done.4.a_got
  34.2 0.1 first_x_sum.1
  34.4 0.4 collective-permute-start.7
  34.8 2.3 %collective-permute-start.6 = (bf16[528,128]{1,0:T(8,128)(2,1)S(1)}, bf16[528,128]{1,0:T(8,128)(2,1)S(1)}, u32[]{:S(2)}, u32[]{:S(2)}) collective-permute-start(bf16[528,128]{1,0:T(8,128)(2,1)S(1)} %get-tuple-element.59), channel_id=1, source_target_pairs={{0,6},{2,4},{4,2},{6,0},{1,7},{3,5},{5,3},{7,1},{8,14},{10,12},{12... | collective-permute-start | bytes 405512 | tf_op jit(solution)/shard_map/ppermute | solution.py:348
  37.1 0.0 collective-permute-done.8
  37.2 0.0 collective-permute-done.9
  37.2 0.0 collective-permute-done.10
  37.2 0.0 copy-done.3
  37.2 0.9 %add_convert_fusion = bf16[4,8,8,512]{3,2,1,0:T(8,128)(2,1)} fusion(bf16[4,8,8,512]{3,2,1,0:T(8,128)(2,1)S(1)} %copy-done.3, bf16[4,4,4,512]{3,2,1,0:T(4,128)(2,1)S(1)} %get-tuple-element.66, bf16[4,4,4,512]{3,2,1,0:T(4,128)(2,1)S(1)} %collective-permute-done.10, bf16[4,4,4,512]{3,2,1,0:T(4,128)(2,1)S(1)} %collective-permute-done.9, ...), kind=kLoop, calls=%fused_computation.1 | loop fusion | flops 1441792 | bytes 786432 | tf_op jit(solution)/shard_map/convert_element_type | solution.py:372
  38.0 1.4 %collective-permute-done.7.b_got = bf16[512,128]{1,0:T(8,128)(2,1)S(1)} collective-permute-done((bf16[512,128]{1,0:T(8,128)(2,1)S(1)}, bf16[512,128]{1,0:T(8,128)(2,1)S(1)}, u32[]{:S(2)}, u32[]{:S(2)}) %collective-permute-start.7) | collective-permute-done | bytes 131104 | tf_op jit(solution)/shard_map/ppermute | solution.py:348
  39.4 1.6 %collective-permute-done.6.a_got = bf16[528,128]{1,0:T(8,128)(2,1)S(1)} collective-permute-done((bf16[528,128]{1,0:T(8,128)(2,1)S(1)}, bf16[528,128]{1,0:T(8,128)(2,1)S(1)}, u32[]{:S(2)}, u32[]{:S(2)}) %collective-permute-start.6) | collective-permute-done | bytes 135200 | tf_op jit(solution)/shard_map/ppermute | solution.py:348
  41.0 0.1 second_x_sum.1
  41.1 21.0 %all_to_all.5.in_ref = bf16[32,9,4,128]{3,2,1,0:T(4,128)(2,1)S(1)} all-to-all(bf16[32,9,4,128]{3,2,1,0:T(4,128)(2,1)S(1)} %second_x_sum.1), channel_id=1, replica_groups=mesh['z'=8,'yh'=2,'c'=2,'x'=4,'yl'=2] {'z','yh','yl'}, dimensions={0} | all-to-all | bytes 589824 | tf_op jit(solution)/shard_map/all_to_all | solution.py:390
  62.2 1.3 %last_sum.1 = (f32[16,192]{1,0:T(8,128)}, f32[16,64]{1,0:T(8,128)}, f32[4,128]{1,0:T(4,128)}) custom-call(s32[4]{0:T(128)S(1)} %pad_add_fusion.place, bf16[32,9,4,128]{3,2,1,0:T(4,128)(2,1)S(1)} %all_to_all.5.in_ref), custom_call_target="tpu_custom_call" | custom-call | tf_op jit(solution)/shard_map/last_sum/pallas_call | solution.py:391
  (4 shorter events, 0.1 us)
Async XLA Ops:
  1.8 10.7 %collective-permute-start = (bf16[2,4,4,4,512]{4,3,2,1,0:T(4,128)(2,1)S(1)}, bf16[2,4,4,4,512]{4,3,2,1,0:T(4,128)(2,1)S(1)}, u32[]{:S(2)}, u32[]{:S(2)}) collective-permute-start(bf16[2,4,4,4,512]{4,3,2,1,0:T(4,128)(2,1)S(1)} %get-tuple-element.38), channel_id=1, source_target_pairs={{0,255},{1,248},{2,249},{3,250},{4,251},{5,252},{6,253},{7,254},{8... | collective-permute-start | bytes 393224 | tf_op jit(solution)/shard_map/ppermute | solution.py:283
  9.9 5.0 %collective-permute-start.1 = (bf16[2,4,4,4,512]{4,3,2,1,0:T(4,128)(2,1)S(1)}, bf16[2,4,4,4,512]{4,3,2,1,0:T(4,128)(2,1)S(1)}, u32[]{:S(2)}, u32[]{:S(2)}) collective-permute-start(bf16[2,4,4,4,512]{4,3,2,1,0:T(4,128)(2,1)S(1)} %get-tuple-element.39), channel_id=1, source_target_pairs={{0,7},{1,0},{2,1},{3,2},{4,3},{5,4},{6,5},{7,6},{8,15},{9,8},{10,9... | collective-permute-start | bytes 393224 | tf_op jit(solution)/shard_map/ppermute | solution.py:283
  10.0 4.8 %collective-permute-start.2 = (bf16[2,4,4,4,512]{4,3,2,1,0:T(4,128)(2,1)S(1)}, bf16[2,4,4,4,512]{4,3,2,1,0:T(4,128)(2,1)S(1)}, u32[]{:S(2)}, u32[]{:S(2)}) collective-permute-start(bf16[2,4,4,4,512]{4,3,2,1,0:T(4,128)(2,1)S(1)} %get-tuple-element.40), channel_id=1, source_target_pairs={{0,248},{1,249},{2,250},{3,251},{4,252},{5,253},{6,254},{7,255},{8... | collective-permute-start | bytes 393224 | tf_op jit(solution)/shard_map/ppermute | solution.py:283
  12.3 2.9 %copy-start = (bf16[512,1536]{1,0:T(8,128)(2,1)S(1)}, bf16[512,1536]{1,0:T(8,128)(2,1)}, u32[]{:S(2)}) copy-start(bf16[512,1536]{1,0:T(8,128)(2,1)} %wqkv_ref.3) | copy-start | bytes 4718596
  12.3 2.9 %copy-start.2 = (f32[512]{0:T(512)S(1)}, f32[512]{0:T(512)}, u32[]{:S(2)}) copy-start(f32[512]{0:T(512)} %param.7) | copy-start | bytes 6148
  15.2 1.2 %copy-start.1 = (bf16[512,512]{1,0:T(8,128)(2,1)S(1)}, bf16[512,512]{1,0:T(8,128)(2,1)}, u32[]{:S(2)}) copy-start(bf16[512,512]{1,0:T(8,128)(2,1)} %wout_ref.1) | copy-start | bytes 1572868
  21.3 2.8 %collective-permute-start.3 = (bf16[4,1040,128]{2,1,0:T(8,128)(2,1)S(1)}, bf16[4,1040,128]{2,1,0:T(8,128)(2,1)S(1)}, u32[]{:S(2)}, u32[]{:S(2)}) collective-permute-start(bf16[4,1040,128]{2,1,0:T(8,128)(2,1)S(1)} %get-tuple-element.50), channel_id=1, source_target_pairs={{0,8},{8,0},{1,9},{9,1},{2,10},{10,2},{3,11},{11,3},{4,12},{12,4},... | collective-permute-start | bytes 3194888 | tf_op jit(solution)/shard_map/ppermute | solution.py:337
  24.3 12.9 %copy-start.3 = (bf16[4,8,8,512]{3,2,1,0:T(8,128)(2,1)S(1)}, bf16[4,8,8,512]{3,2,1,0:T(8,128)(2,1)}, u32[]{:S(2)}) copy-start(bf16[4,8,8,512]{3,2,1,0:T(8,128)(2,1)} %dy_ref.1) | copy-start | bytes 786436
  24.3 9.9 %collective-permute-start.4 = (bf16[2,528,128]{2,1,0:T(8,128)(2,1)S(1)}, bf16[2,528,128]{2,1,0:T(8,128)(2,1)S(1)}, u32[]{:S(2)}, u32[]{:S(2)}) collective-permute-start(bf16[2,528,128]{2,1,0:T(8,128)(2,1)S(1)} %get-tuple-element.55), channel_id=1, source_target_pairs={{0,2},{2,0},{4,6},{6,4},{1,3},{3,1},{5,7},{7,5},{8,10},{10,8},{12,... | collective-permute-start | bytes 811016 | tf_op jit(solution)/shard_map/ppermute | solution.py:348
  24.9 9.3 %collective-permute-start.5 = (bf16[2,512,128]{2,1,0:T(8,128)(2,1)S(1)}, bf16[2,512,128]{2,1,0:T(8,128)(2,1)S(1)}, u32[]{:S(2)}, u32[]{:S(2)}) collective-permute-start(bf16[2,512,128]{2,1,0:T(8,128)(2,1)S(1)} %get-tuple-element.57), channel_id=1, source_target_pairs={{0,6},{2,4},{4,2},{6,0},{1,7},{3,5},{5,3},{7,1},{8,14},{10,12},{12... | collective-permute-start | bytes 786440 | tf_op jit(solution)/shard_map/ppermute | solution.py:348
  27.2 10.0 %collective-permute-start.8 = (bf16[4,4,4,512]{3,2,1,0:T(4,128)(2,1)S(1)}, bf16[4,4,4,512]{3,2,1,0:T(4,128)(2,1)S(1)}, u32[]{:S(2)}, u32[]{:S(2)}) collective-permute-start(bf16[4,4,4,512]{3,2,1,0:T(4,128)(2,1)S(1)} %get-tuple-element.63), channel_id=1, source_target_pairs={{0,9},{1,10},{2,11},{3,12},{4,13},{5,14},{6,15},{7,8},{8,17},{9,18... | collective-permute-start | bytes 196616 | tf_op jit(solution)/shard_map/ppermute | solution.py:283
  27.3 9.9 %collective-permute-start.9 = (bf16[4,4,4,512]{3,2,1,0:T(4,128)(2,1)S(1)}, bf16[4,4,4,512]{3,2,1,0:T(4,128)(2,1)S(1)}, u32[]{:S(2)}, u32[]{:S(2)}) collective-permute-start(bf16[4,4,4,512]{3,2,1,0:T(4,128)(2,1)S(1)} %get-tuple-element.64), channel_id=1, source_target_pairs={{0,1},{1,2},{2,3},{3,4},{4,5},{5,6},{6,7},{7,0},{8,9},{9,10},{10,1... | collective-permute-start | bytes 196616 | tf_op jit(solution)/shard_map/ppermute | solution.py:283
  29.2 8.0 %collective-permute-start.10 = (bf16[4,4,4,512]{3,2,1,0:T(4,128)(2,1)S(1)}, bf16[4,4,4,512]{3,2,1,0:T(4,128)(2,1)S(1)}, u32[]{:S(2)}, u32[]{:S(2)}) collective-permute-start(bf16[4,4,4,512]{3,2,1,0:T(4,128)(2,1)S(1)} %get-tuple-element.65), channel_id=1, source_target_pairs={{0,8},{1,9},{2,10},{3,11},{4,12},{5,13},{6,14},{7,15},{8,16},{9,17... | collective-permute-start | bytes 196616 | tf_op jit(solution)/shard_map/ppermute | solution.py:283
  34.4 5.1 %collective-permute-start.7 = (bf16[512,128]{1,0:T(8,128)(2,1)S(1)}, bf16[512,128]{1,0:T(8,128)(2,1)S(1)}, u32[]{:S(2)}, u32[]{:S(2)}) collective-permute-start(bf16[512,128]{1,0:T(8,128)(2,1)S(1)} %get-tuple-element.61), channel_id=1, source_target_pairs={{0,2},{2,0},{4,6},{6,4},{1,3},{3,1},{5,7},{7,5},{8,10},{10,8},{12,... | collective-permute-start | bytes 393224 | tf_op jit(solution)/shard_map/ppermute | solution.py:348
  34.8 6.2 %collective-permute-start.6 = (bf16[528,128]{1,0:T(8,128)(2,1)S(1)}, bf16[528,128]{1,0:T(8,128)(2,1)S(1)}, u32[]{:S(2)}, u32[]{:S(2)}) collective-permute-start(bf16[528,128]{1,0:T(8,128)(2,1)S(1)} %get-tuple-element.59), channel_id=1, source_target_pairs={{0,6},{2,4},{4,2},{6,0},{1,7},{3,5},{5,3},{7,1},{8,14},{10,12},{12... | collective-permute-start | bytes 405512 | tf_op jit(solution)/shard_map/ppermute | solution.py:348

commit v2 on v1

--- a/solution.py
+++ b/solution.py
@@ -55,14 +55,33 @@
     return (iota((128, 128), 0) // HD == iota((128, 128), 1) // HD).astype(F32).astype(BF16)
 
 
+def fetch_kernel(wqkv_ref, wout_ref, wqkv_out, wout_out, sems):
+    copies = [
+        pltpu.make_async_copy(wqkv_ref, wqkv_out, sems.at[0]),
+        pltpu.make_async_copy(wout_ref, wout_out, sems.at[1]),
+    ]
+    for copy in copies:
+        copy.start()
+    for copy in copies:
+        copy.wait()
+
+
 def forward_kernel(
-    x_ref, gain_ref, wqkv_ref, cos_ref, sin_ref,
-    n_ref, qk_ref, v_ref, scale_ref, qkv_ref,
+    diag_ref, east_ref, below_ref, own_ref, gain_ref, wqkv_ref, cos_ref, sin_ref,
+    x_ref, dy_ref, n_ref, qk_ref, v_ref, scale_ref, qkv_ref,
 ):
     gain = gain_ref[...]
+
+    def window(j, w):
+        top = jnp.concatenate([diag_ref[j, w].astype(F32), below_ref[j, w].astype(F32)], 1)
+        low = jnp.concatenate([east_ref[j, w].astype(F32), own_ref[j, w].astype(F32)], 1)
+        return jnp.concatenate([top, low], 0).reshape(64, 512)
+
     for w in range(4):
         rows = slice(64 * w, 64 * w + 64)
-        xs = x_ref[rows, :].astype(F32)
+        dy_ref[rows, :] = window(1, w).astype(BF16)
+        xs = window(0, w)
+        x_ref[rows, :] = xs.astype(BF16)
         inv = lax.rsqrt(jnp.mean(xs * xs, -1, keepdims=True) + 1e-05)
         n_ref[rows, :] = (xs * inv * gain).astype(BF16)
     qkv_ref[...] = mm(n_ref[...], wqkv_ref[...])
@@ -185,7 +204,8 @@
         for j, part in enumerate(parts):
             part = part.astype(BF16)
             for i in range(16):
-                at_row = 16 + 64 * i + 16 * j
+                block = (i % 2 * 2 + j // 2) * 8 + i // 2
+                at_row = 16 + 32 * block + 16 * (j % 2)
                 out_ref[rel, at_row : at_row + 16, :] = part[16 * i : 16 * i + 16, :]
         out_ref[rel, 0:16, :] = tail
 
@@ -292,11 +312,16 @@
         name="quads",
     )(*(pltpu.with_memory_space_constraint(v, pltpu.HBM) for v in (tokens, cotangent)))
     diag, east, below = send(diag, -1, -1), send(east, -1, 0), send(below, 0, -1)
-    win = jnp.concatenate(
-        [jnp.concatenate([diag, below], 3), jnp.concatenate([east, own], 3)], 2
-    )
-    xw = win[0].reshape(256, 512)
-    dyw = win[1].reshape(256, 512)
+    w_qkv, w_out = pl.pallas_call(
+        fetch_kernel,
+        out_shape=(shape((512, 1536)), shape((512, 512))),
+        in_specs=[pl.BlockSpec(memory_space=pl.ANY)] * 2,
+        out_specs=(VMEM,) * 2,
+        scratch_shapes=[pltpu.SemaphoreType.DMA((2,))],
+        compiler_params=PARAMS,
+        cost_estimate=pl.CostEstimate(flops=0, bytes_accessed=4_000_000, transcendentals=0),
+        name="fetch_weights",
+    )(*(pltpu.with_memory_space_constraint(v, pltpu.HBM) for v in (w_qkv, w_out)))
 
     cell = jnp.arange(64, dtype=jnp.int32)[:, None]
     entry = jnp.arange(128, dtype=jnp.int32)[None, :]
@@ -309,18 +334,18 @@
     sine = jnp.sin(angle) * jnp.where(entry % HD < 16, -1.0, 1.0)
 
     gain_row = norm_gain.reshape(1, 512)
-    normed, qk, value, scales = pl.pallas_call(
+    xw, dyw, normed, qk, value, scales = pl.pallas_call(
         forward_kernel,
-        out_shape=(
-            shape((256, 512)), shape((256, 1024)), shape((256, 512)), shape((256, 1024), F32),
+        out_shape=(shape((256, 512)),) * 3 + (
+            shape((256, 1024)), shape((256, 512)), shape((256, 1024), F32),
         ),
-        in_specs=[VMEM] * 5,
-        out_specs=(VMEM,) * 4,
+        in_specs=[VMEM] * 8,
+        out_specs=(VMEM,) * 6,
         scratch_shapes=[pltpu.VMEM((256, 1536), F32)],
         compiler_params=PARAMS,
         cost_estimate=pl.CostEstimate(flops=400_000_000, bytes_accessed=5_000_000, transcendentals=0),
         name="window_forward",
-    )(xw, gain_row, w_qkv, cosine, sine)
+    )(diag, east, below, own, gain_row, w_qkv, cosine, sine)
     give, dqkv, dn, nt, at, tail = pl.pallas_call(
         backward_kernel,
         out_shape=(
@@ -387,7 +412,7 @@
         name="second_x_sum",
     )(a_mine, along_x(a_give, 3), b_mine, along_x(b_give, 1))
     parts, grad_tokens = lax.optimization_barrier((parts, grad_tokens))
-    parts = lax.all_to_all(parts, ("z", "yh", "yl"), 0, 0, tiled=True)
+    parts = lax.all_to_all(parts, ("yh", "yl", "z"), 0, 0, tiled=True)
     qkv_share, out_share, gain_share = pl.pallas_call(
         last_kernel,
         out_shape=(shape((16, 192), F32), shape((16, 64), F32), shape((4, 128), F32)),

time: 63.7 us -> 63.1 us (level)
  blocking collectives: 21 us -> 18.7 us
  Pallas kernels: 10.5 us -> 12 us
    all_to_all x1, blocking collectives: 21 us -> 18.7 us  [per_device(): parts = lax.all_to_all(parts, ('yh', 'yl', 'z'), 0, 0, tiled=True)]
    pallas_call x1 -> x2, Pallas kernels: 1.13 us -> 2.7 us  [the longest x1 1.54 us: per_device(): pl.pallas_call(fetch_kernel, out_shape=(shape((512, 1536)), shape((512, 5...]
  transfers between devices with their start and end apart: 11 -> 11, of which waited for: 5 -> 6; matrix products, arithmetic and copies ran while one was open for 2% -> 2% of each run, Pallas kernels for 3% -> 5%
where the time goes in v2:
time: 63.1 us; the launch traced here: 62.5 us
  blocking collectives  18.7 us (30%)
  starting transfers between devices  17.4 us (28%)
  waiting for transfers between devices  12.5 us (20%)
  Pallas kernels  12 us (19%)
  other arithmetic  1.17 us (2%)
  between operations  0.75 us (1%)
    all_to_all x1, blocking collectives, per_device(): parts = lax.all_to_all(parts, ('yh', 'yl', 'z'), 0, 0, tiled=True)  18.7 us
    ppermute x6, starting transfers between devices, send(): return lax.ppermute(v, every, pairs)  11.9 us
    ppermute x4, waiting for transfers between devices, along_x(): return lax.ppermute(v, 'x', [(i, i ^ mask) for i in range(4)])  8.05 us
    ppermute x4, starting transfers between devices, along_x(): return lax.ppermute(v, 'x', [(i, i ^ mask) for i in range(4)])  5.38 us
    pallas_call x1, Pallas kernels, per_device(): pl.pallas_call(backward_kernel, out_shape=(shape((4, ROWS, 128)), shape((...  4.9 us
    ppermute x6, waiting for transfers between devices, send(): return lax.ppermute(v, every, pairs)  2.96 us
    pallas_call x1, Pallas kernels, per_device(): pl.pallas_call(fetch_kernel, out_shape=(shape((512, 1536)), shape((512, 5...  1.54 us
    ppermute x1, waiting for transfers between devices, per_device(): got = lax.ppermute(give, 'c', [(0, 1), (1, 0)])  1.48 us
  transfers between devices with their start and end apart: 11, of which 6 were waited for; matrix products, arithmetic and copies ran while one was open for 2% of the time, Pallas kernels for 5%

profile of v2, /device:TPU:6, one launch (start us, length us, event | category | flops | bytes accessed | tf_op | source)
XLA Modules:
  0.0 62.5 jit_solution(5470289817719602556)
XLA Ops:
  0.6 1.1 %quads.1 = (bf16[2,4,4,4,512]{4,3,2,1,0:T(4,128)(2,1)S(1)}, bf16[2,4,4,4,512]{4,3,2,1,0:T(4,128)(2,1)S(1)}, bf16[2,4,4,4,512]{4,3,2,1,0:T(4,128)(2,1)S(1)}, bf16[2,4,4,4,512]{4,3,2,1,0:T(4,128)(2,1)S(1)}) custom-call(bf16[4,8,8,512]{3,2,1,0:T(8,128)(2,1)} %x_ref.1, bf16[4,8,8,512]{3,2,1,0:T(8,128)(2,1)} %dy_ref.1), custom_call_target="tpu_custom_call" | custom-call | tf_op jit(solution)/shard_map/quads/pallas_call | solution.py:305
  1.8 8.1 %collective-permute-start = (bf16[2,4,4,4,512]{4,3,2,1,0:T(4,128)(2,1)S(1)}, bf16[2,4,4,4,512]{4,3,2,1,0:T(4,128)(2,1)S(1)}, u32[]{:S(2)}, u32[]{:S(2)}) collective-permute-start(bf16[2,4,4,4,512]{4,3,2,1,0:T(4,128)(2,1)S(1)} %get-tuple-element.42), channel_id=1, source_target_pairs={{0,255},{1,248},{2,249},{3,250},{4,251},{5,252},{6,253},{7,254},{8... | collective-permute-start | bytes 393224 | tf_op jit(solution)/shard_map/ppermute | solution.py:303
  9.9 1.7 %collective-permute-start.1 = (bf16[2,4,4,4,512]{4,3,2,1,0:T(4,128)(2,1)S(1)}, bf16[2,4,4,4,512]{4,3,2,1,0:T(4,128)(2,1)S(1)}, u32[]{:S(2)}, u32[]{:S(2)}) collective-permute-start(bf16[2,4,4,4,512]{4,3,2,1,0:T(4,128)(2,1)S(1)} %get-tuple-element.43), channel_id=1, source_target_pairs={{0,248},{1,249},{2,250},{3,251},{4,252},{5,253},{6,254},{7,255},{8... | collective-permute-start | bytes 393224 | tf_op jit(solution)/shard_map/ppermute | solution.py:303
  11.6 0.1 collective-permute-start.2
  11.8 0.2 sine_multiply_fusion
  12.0 0.0 copy-start
  12.0 1.5 %fetch_weights.1 = (bf16[512,1536]{1,0:T(8,128)(2,1)S(1)}, bf16[512,512]{1,0:T(8,128)(2,1)S(1)}) custom-call(bf16[512,1536]{1,0:T(8,128)(2,1)} %wqkv_ref.1, bf16[512,512]{1,0:T(8,128)(2,1)} %wout_ref.1), custom_call_target="tpu_custom_call" | custom-call | bytes 4000000 | tf_op jit(solution)/shard_map/fetch_weights/pallas_call | solution.py:315
  13.6 0.1 pad_add_fusion.place
  13.6 0.0 collective-permute-done.diag_ref
  13.6 0.5 collective-permute-done.1.east_ref
  14.1 2.4 %collective-permute-done.2.below_ref = bf16[2,4,4,4,512]{4,3,2,1,0:T(4,128)(2,1)S(1)} collective-permute-done((bf16[2,4,4,4,512]{4,3,2,1,0:T(4,128)(2,1)S(1)}, bf16[2,4,4,4,512]{4,3,2,1,0:T(4,128)(2,1)S(1)}, u32[]{:S(2)}, u32[]{:S(2)}) %collective-permute-start.2) | collective-permute-done | bytes 131104 | tf_op jit(solution)/shard_map/ppermute | solution.py:303
  16.6 0.0 copy-done
  16.6 1.2 %window_forward.1 = (bf16[256,512]{1,0:T(8,128)(2,1)S(1)}, bf16[256,512]{1,0:T(8,128)(2,1)S(1)}, bf16[256,512]{1,0:T(8,128)(2,1)S(1)}, bf16[256,1024]{1,0:T(8,12...) custom-call(bf16[2,4,4,4,512]{4,3,2,1,0:T(4,128)(2,1)S(1)} %collective-permute-done.diag_ref, ...), custom_call_target="tpu_custom_call" | custom-call | flops 400000000 | bytes 5000000 | tf_op jit(solution)/shard_map/window_forward/pallas_call | solution.py:337
  17.8 4.9 %window_backward.1 = (bf16[4,1040,128]{2,1,0:T(8,128)(2,1)S(1)}, bf16[256,1536]{1,0:T(8,128)(2,1)S(1)}, f32[256,512]{1,0:T(8,128)S(1)}, bf16[16,2,16,256]{3,2,1,...) custom-call(s32[4]{0:T(128)S(1)} %pad_add_fusion.place, ...), custom_call_target="tpu_custom_call" | custom-call | tf_op jit(solution)/shard_map/window_backward/pallas_call | solution.py:349
  22.7 0.1 collective-permute-start.3
  22.8 1.2 %kept_half.1.keep_ref = bf16[4,1040,128]{2,1,0:T(8,128)(2,1)S(1)} custom-call(s32[4]{0:T(128)S(1)} %pad_add_fusion.place, bf16[256,512]{1,0:T(8,128)(2,1)S(1)} %get-tuple-element.47.dy_ref, bf16[256,1536]{1,0:T(8,128)(2,1)S(1)} %get-tuple-element.54.dqkv_ref, bf16[16,2,16,256]{3,2,1,0:T(8,128)(2,1)S(1)} %get-tuple-element.55.nt_ref, ...), custom_call_target="tpu_custom_call" | custom-call | flops 300000000 | bytes 4000000 | tf_op jit(solution)/shard_map/kept_half/pallas_call | solution.py:363
  23.9 1.5 %collective-permute-done.3.got_ref = bf16[4,1040,128]{2,1,0:T(8,128)(2,1)S(1)} collective-permute-done((bf16[4,1040,128]{2,1,0:T(8,128)(2,1)S(1)}, bf16[4,1040,128]{2,1,0:T(8,128)(2,1)S(1)}, u32[]{:S(2)}, u32[]{:S(2)}) %collective-permute-start.3) | collective-permute-done | bytes 1064992 | tf_op jit(solution)/shard_map/ppermute | solution.py:362
  25.4 0.3 pair_sum.1
  25.7 0.0 copy-start.1
  25.7 0.6 collective-permute-start.4
  26.3 2.0 %collective-permute-start.5 = (bf16[2,512,128]{2,1,0:T(8,128)(2,1)S(1)}, bf16[2,512,128]{2,1,0:T(8,128)(2,1)S(1)}, u32[]{:S(2)}, u32[]{:S(2)}) collective-permute-start(bf16[2,512,128]{2,1,0:T(8,128)(2,1)S(1)} %get-tuple-element.65), channel_id=1, source_target_pairs={{0,6},{2,4},{4,2},{6,0},{1,7},{3,5},{5,3},{7,1},{8,14},{10,12},{12... | collective-permute-start | bytes 786440 | tf_op jit(solution)/shard_map/ppermute | solution.py:373
  28.3 0.2 norm_backward.1
  28.5 0.1 collective-permute-start.8
  28.6 1.9 %collective-permute-start.9 = (bf16[4,4,4,512]{3,2,1,0:T(4,128)(2,1)S(1)}, bf16[4,4,4,512]{3,2,1,0:T(4,128)(2,1)S(1)}, u32[]{:S(2)}, u32[]{:S(2)}) collective-permute-start(bf16[4,4,4,512]{3,2,1,0:T(4,128)(2,1)S(1)} %get-tuple-element.72), channel_id=1, source_target_pairs={{0,1},{1,2},{2,3},{3,4},{4,5},{5,6},{6,7},{7,0},{8,9},{9,10},{10,1... | collective-permute-start | bytes 196616 | tf_op jit(solution)/shard_map/ppermute | solution.py:303
  30.5 0.0 collective-permute-start.10
  30.5 5.1 %collective-permute-done.5.b_got = bf16[2,512,128]{2,1,0:T(8,128)(2,1)S(1)} collective-permute-done((bf16[2,512,128]{2,1,0:T(8,128)(2,1)S(1)}, bf16[2,512,128]{2,1,0:T(8,128)(2,1)S(1)}, u32[]{:S(2)}, u32[]{:S(2)}) %collective-permute-start.5) | collective-permute-done | bytes 262176 | tf_op jit(solution)/shard_map/ppermute | solution.py:373
  35.6 0.0 collective-permute-done.4.a_got
  35.6 0.1 first_x_sum.1
  35.7 0.4 collective-permute-start.7
  36.2 2.3 %collective-permute-start.6 = (bf16[528,128]{1,0:T(8,128)(2,1)S(1)}, bf16[528,128]{1,0:T(8,128)(2,1)S(1)}, u32[]{:S(2)}, u32[]{:S(2)}) collective-permute-start(bf16[528,128]{1,0:T(8,128)(2,1)S(1)} %get-tuple-element.67), channel_id=1, source_target_pairs={{0,6},{2,4},{4,2},{6,0},{1,7},{3,5},{5,3},{7,1},{8,14},{10,12},{12... | collective-permute-start | bytes 405512 | tf_op jit(solution)/shard_map/ppermute | solution.py:373
  38.5 0.0 collective-permute-done.8
  38.5 0.0 collective-permute-done.9
  38.5 0.0 collective-permute-done.10
  38.5 0.0 copy-done.1
  38.5 0.9 %add_convert_fusion = bf16[4,8,8,512]{3,2,1,0:T(8,128)(2,1)} fusion(bf16[4,8,8,512]{3,2,1,0:T(8,128)(2,1)S(1)} %copy-done.1, bf16[4,4,4,512]{3,2,1,0:T(4,128)(2,1)S(1)} %get-tuple-element.74, bf16[4,4,4,512]{3,2,1,0:T(4,128)(2,1)S(1)} %collective-permute-done.10, bf16[4,4,4,512]{3,2,1,0:T(4,128)(2,1)S(1)} %collective-permute-done.9, ...), kind=kLoop, calls=%fused_computation | loop fusion | flops 1441792 | bytes 786432 | tf_op jit(solution)/shard_map/convert_element_type | solution.py:397
  39.4 1.4 %collective-permute-done.7.b_got = bf16[512,128]{1,0:T(8,128)(2,1)S(1)} collective-permute-done((bf16[512,128]{1,0:T(8,128)(2,1)S(1)}, bf16[512,128]{1,0:T(8,128)(2,1)S(1)}, u32[]{:S(2)}, u32[]{:S(2)}) %collective-permute-start.7) | collective-permute-done | bytes 131104 | tf_op jit(solution)/shard_map/ppermute | solution.py:373
  40.8 1.6 %collective-permute-done.6.a_got = bf16[528,128]{1,0:T(8,128)(2,1)S(1)} collective-permute-done((bf16[528,128]{1,0:T(8,128)(2,1)S(1)}, bf16[528,128]{1,0:T(8,128)(2,1)S(1)}, u32[]{:S(2)}, u32[]{:S(2)}) %collective-permute-start.6) | collective-permute-done | bytes 135200 | tf_op jit(solution)/shard_map/ppermute | solution.py:373
  42.4 0.1 second_x_sum.1
  42.5 18.7 %all_to_all.5.in_ref = bf16[32,9,4,128]{3,2,1,0:T(4,128)(2,1)S(1)} all-to-all(bf16[32,9,4,128]{3,2,1,0:T(4,128)(2,1)S(1)} %second_x_sum.1), channel_id=1, replica_groups=mesh['z'=8,'yh'=2,'c'=2,'x'=4,'yl'=2] {'yh','yl','z'}, dimensions={0} | all-to-all | bytes 589824 | tf_op jit(solution)/shard_map/all_to_all | solution.py:415
  61.2 1.3 %last_sum.1 = (f32[16,192]{1,0:T(8,128)}, f32[16,64]{1,0:T(8,128)}, f32[4,128]{1,0:T(4,128)}) custom-call(s32[4]{0:T(128)S(1)} %pad_add_fusion.place, bf16[32,9,4,128]{3,2,1,0:T(4,128)(2,1)S(1)} %all_to_all.5.in_ref), custom_call_target="tpu_custom_call" | custom-call | tf_op jit(solution)/shard_map/last_sum/pallas_call | solution.py:416
  (3 shorter events, 0.0 us)
Async XLA Ops:
  1.8 11.9 %collective-permute-start = (bf16[2,4,4,4,512]{4,3,2,1,0:T(4,128)(2,1)S(1)}, bf16[2,4,4,4,512]{4,3,2,1,0:T(4,128)(2,1)S(1)}, u32[]{:S(2)}, u32[]{:S(2)}) collective-permute-start(bf16[2,4,4,4,512]{4,3,2,1,0:T(4,128)(2,1)S(1)} %get-tuple-element.42), channel_id=1, source_target_pairs={{0,255},{1,248},{2,249},{3,250},{4,251},{5,252},{6,253},{7,254},{8... | collective-permute-start | bytes 393224 | tf_op jit(solution)/shard_map/ppermute | solution.py:303
  9.9 4.3 %collective-permute-start.1 = (bf16[2,4,4,4,512]{4,3,2,1,0:T(4,128)(2,1)S(1)}, bf16[2,4,4,4,512]{4,3,2,1,0:T(4,128)(2,1)S(1)}, u32[]{:S(2)}, u32[]{:S(2)}) collective-permute-start(bf16[2,4,4,4,512]{4,3,2,1,0:T(4,128)(2,1)S(1)} %get-tuple-element.43), channel_id=1, source_target_pairs={{0,248},{1,249},{2,250},{3,251},{4,252},{5,253},{6,254},{7,255},{8... | collective-permute-start | bytes 393224 | tf_op jit(solution)/shard_map/ppermute | solution.py:303
  11.6 5.0 %collective-permute-start.2 = (bf16[2,4,4,4,512]{4,3,2,1,0:T(4,128)(2,1)S(1)}, bf16[2,4,4,4,512]{4,3,2,1,0:T(4,128)(2,1)S(1)}, u32[]{:S(2)}, u32[]{:S(2)}) collective-permute-start(bf16[2,4,4,4,512]{4,3,2,1,0:T(4,128)(2,1)S(1)} %get-tuple-element.44), channel_id=1, source_target_pairs={{0,7},{1,0},{2,1},{3,2},{4,3},{5,4},{6,5},{7,6},{8,15},{9,8},{10,9... | collective-permute-start | bytes 393224 | tf_op jit(solution)/shard_map/ppermute | solution.py:303
  12.0 4.6 %copy-start = (f32[512]{0:T(512)S(1)}, f32[512]{0:T(512)}, u32[]{:S(2)}) copy-start(f32[512]{0:T(512)} %param.7) | copy-start | bytes 6148
  22.7 2.8 %collective-permute-start.3 = (bf16[4,1040,128]{2,1,0:T(8,128)(2,1)S(1)}, bf16[4,1040,128]{2,1,0:T(8,128)(2,1)S(1)}, u32[]{:S(2)}, u32[]{:S(2)}) collective-permute-start(bf16[4,1040,128]{2,1,0:T(8,128)(2,1)S(1)} %get-tuple-element.58), channel_id=1, source_target_pairs={{0,8},{8,0},{1,9},{9,1},{2,10},{10,2},{3,11},{11,3},{4,12},{12,4},... | collective-permute-start | bytes 3194888 | tf_op jit(solution)/shard_map/ppermute | solution.py:362
  25.7 12.9 %copy-start.1 = (bf16[4,8,8,512]{3,2,1,0:T(8,128)(2,1)S(1)}, bf16[4,8,8,512]{3,2,1,0:T(8,128)(2,1)}, u32[]{:S(2)}) copy-start(bf16[4,8,8,512]{3,2,1,0:T(8,128)(2,1)} %dy_ref.1) | copy-start | bytes 786436
  25.7 9.9 %collective-permute-start.4 = (bf16[2,528,128]{2,1,0:T(8,128)(2,1)S(1)}, bf16[2,528,128]{2,1,0:T(8,128)(2,1)S(1)}, u32[]{:S(2)}, u32[]{:S(2)}) collective-permute-start(bf16[2,528,128]{2,1,0:T(8,128)(2,1)S(1)} %get-tuple-element.63), channel_id=1, source_target_pairs={{0,2},{2,0},{4,6},{6,4},{1,3},{3,1},{5,7},{7,5},{8,10},{10,8},{12,... | collective-permute-start | bytes 811016 | tf_op jit(solution)/shard_map/ppermute | solution.py:373
  26.3 9.3 %collective-permute-start.5 = (bf16[2,512,128]{2,1,0:T(8,128)(2,1)S(1)}, bf16[2,512,128]{2,1,0:T(8,128)(2,1)S(1)}, u32[]{:S(2)}, u32[]{:S(2)}) collective-permute-start(bf16[2,512,128]{2,1,0:T(8,128)(2,1)S(1)} %get-tuple-element.65), channel_id=1, source_target_pairs={{0,6},{2,4},{4,2},{6,0},{1,7},{3,5},{5,3},{7,1},{8,14},{10,12},{12... | collective-permute-start | bytes 786440 | tf_op jit(solution)/shard_map/ppermute | solution.py:373
  28.5 10.0 %collective-permute-start.8 = (bf16[4,4,4,512]{3,2,1,0:T(4,128)(2,1)S(1)}, bf16[4,4,4,512]{3,2,1,0:T(4,128)(2,1)S(1)}, u32[]{:S(2)}, u32[]{:S(2)}) collective-permute-start(bf16[4,4,4,512]{3,2,1,0:T(4,128)(2,1)S(1)} %get-tuple-element.71), channel_id=1, source_target_pairs={{0,9},{1,10},{2,11},{3,12},{4,13},{5,14},{6,15},{7,8},{8,17},{9,18... | collective-permute-start | bytes 196616 | tf_op jit(solution)/shard_map/ppermute | solution.py:303
  28.6 9.9 %collective-permute-start.9 = (bf16[4,4,4,512]{3,2,1,0:T(4,128)(2,1)S(1)}, bf16[4,4,4,512]{3,2,1,0:T(4,128)(2,1)S(1)}, u32[]{:S(2)}, u32[]{:S(2)}) collective-permute-start(bf16[4,4,4,512]{3,2,1,0:T(4,128)(2,1)S(1)} %get-tuple-element.72), channel_id=1, source_target_pairs={{0,1},{1,2},{2,3},{3,4},{4,5},{5,6},{6,7},{7,0},{8,9},{9,10},{10,1... | collective-permute-start | bytes 196616 | tf_op jit(solution)/shard_map/ppermute | solution.py:303
  30.5 8.0 %collective-permute-start.10 = (bf16[4,4,4,512]{3,2,1,0:T(4,128)(2,1)S(1)}, bf16[4,4,4,512]{3,2,1,0:T(4,128)(2,1)S(1)}, u32[]{:S(2)}, u32[]{:S(2)}) collective-permute-start(bf16[4,4,4,512]{3,2,1,0:T(4,128)(2,1)S(1)} %get-tuple-element.73), channel_id=1, source_target_pairs={{0,8},{1,9},{2,10},{3,11},{4,12},{5,13},{6,14},{7,15},{8,16},{9,17... | collective-permute-start | bytes 196616 | tf_op jit(solution)/shard_map/ppermute | solution.py:303
  35.7 5.1 %collective-permute-start.7 = (bf16[512,128]{1,0:T(8,128)(2,1)S(1)}, bf16[512,128]{1,0:T(8,128)(2,1)S(1)}, u32[]{:S(2)}, u32[]{:S(2)}) collective-permute-start(bf16[512,128]{1,0:T(8,128)(2,1)S(1)} %get-tuple-element.69), channel_id=1, source_target_pairs={{0,2},{2,0},{4,6},{6,4},{1,3},{3,1},{5,7},{7,5},{8,10},{10,8},{12,... | collective-permute-start | bytes 393224 | tf_op jit(solution)/shard_map/ppermute | solution.py:373
  36.2 6.2 %collective-permute-start.6 = (bf16[528,128]{1,0:T(8,128)(2,1)S(1)}, bf16[528,128]{1,0:T(8,128)(2,1)S(1)}, u32[]{:S(2)}, u32[]{:S(2)}) collective-permute-start(bf16[528,128]{1,0:T(8,128)(2,1)S(1)} %get-tuple-element.67), channel_id=1, source_target_pairs={{0,6},{2,4},{4,2},{6,0},{1,7},{3,5},{5,3},{7,1},{8,14},{10,12},{12... | collective-permute-start | bytes 405512 | tf_op jit(solution)/shard_map/ppermute | solution.py:373

commit v3 on v2

--- a/solution.py
+++ b/solution.py
@@ -67,8 +67,8 @@
 
 
 def forward_kernel(
-    diag_ref, east_ref, below_ref, own_ref, gain_ref, wqkv_ref, cos_ref, sin_ref,
-    x_ref, dy_ref, n_ref, qk_ref, v_ref, scale_ref, qkv_ref,
+    diag_ref, east_ref, below_ref, own_ref, gain_ref, wqkv_ref, wout_ref, cos_ref, sin_ref,
+    x_ref, dy_ref, n_ref, qk_ref, v_ref, scale_ref, qkv_ref, da_ref,
 ):
     gain = gain_ref[...]
 
@@ -85,6 +85,7 @@
         inv = lax.rsqrt(jnp.mean(xs * xs, -1, keepdims=True) + 1e-05)
         n_ref[rows, :] = (xs * inv * gain).astype(BF16)
     qkv_ref[...] = mm(n_ref[...], wqkv_ref[...])
+    da_ref[...] = mt(dy_ref[...], wout_ref[...]).astype(BF16)
     cosine, sine, ones32 = cos_ref[...], sin_ref[...], head_ones()
     for w in range(4):
         rows = slice(64 * w, 64 * w + 64)
@@ -100,12 +101,11 @@
 
 
 def backward_kernel(
-    place, x_ref, dy_ref, wqkv_ref, wout_ref, cos_ref, sin_ref, n_ref, qk_ref, v_ref, scale_ref,
+    place, x_ref, dy_ref, wqkv_ref, cos_ref, sin_ref, n_ref, qk_ref, v_ref, scale_ref,
     send_ref, dqkv_ref, dn_ref, nt_ref, at_ref, tail_ref,
     da_ref, att_ref,
 ):
     core, xpos, capped = place[0], place[1], place[2]
-    da_ref[...] = mt(dy_ref[...], wout_ref[...]).astype(BF16)
 
     lane = iota((64, 128), 1)
     head = [(lane // HD == h).astype(F32).astype(BF16) for h in range(4)]
@@ -186,6 +186,22 @@
     nt_ref[...] = n_ref[...].T.reshape(16, 2, 16, 256)
     at_ref[...] = att_ref[...].T.reshape(16, 2, 16, 256)
     products(send_ref, 1 - core, xpos, nt_ref, at_ref, dqkv_ref, dy_ref, tail)
+
+
+def window_kernel(
+    place, diag_ref, east_ref, below_ref, own_ref, gain_ref, wqkv_ref, wout_ref, cos_ref, sin_ref,
+    x_ref, dy_ref, send_ref, dqkv_ref, dn_ref, nt_ref, at_ref, tail_ref,
+    n_ref, qk_ref, v_ref, scale_ref, qkv_ref, da_ref, att_ref,
+):
+    forward_kernel(
+        diag_ref, east_ref, below_ref, own_ref, gain_ref, wqkv_ref, wout_ref, cos_ref, sin_ref,
+        x_ref, dy_ref, n_ref, qk_ref, v_ref, scale_ref, qkv_ref, da_ref,
+    )
+    backward_kernel(
+        place, x_ref, dy_ref, wqkv_ref, cos_ref, sin_ref, n_ref, qk_ref, v_ref, scale_ref,
+        send_ref, dqkv_ref, dn_ref, nt_ref, at_ref, tail_ref,
+        da_ref, att_ref,
+    )
 
 
 def products(out_ref, half, xpos, nt_ref, at_ref, dqkv_ref, dy_ref, tail):
@@ -334,30 +350,27 @@
     sine = jnp.sin(angle) * jnp.where(entry % HD < 16, -1.0, 1.0)
 
     gain_row = norm_gain.reshape(1, 512)
-    xw, dyw, normed, qk, value, scales = pl.pallas_call(
-        forward_kernel,
-        out_shape=(shape((256, 512)),) * 3 + (
-            shape((256, 1024)), shape((256, 512)), shape((256, 1024), F32),
-        ),
-        in_specs=[VMEM] * 8,
-        out_specs=(VMEM,) * 6,
-        scratch_shapes=[pltpu.VMEM((256, 1536), F32)],
-        compiler_params=PARAMS,
-        cost_estimate=pl.CostEstimate(flops=400_000_000, bytes_accessed=5_000_000, transcendentals=0),
-        name="window_forward",
-    )(diag, east, below, own, gain_row, w_qkv, cosine, sine)
-    give, dqkv, dn, nt, at, tail = pl.pallas_call(
-        backward_kernel,
+    xw, dyw, give, dqkv, dn, nt, at, tail = pl.pallas_call(
+        window_kernel,
         out_shape=(
+            shape((256, 512)), shape((256, 512)),
             shape((4, ROWS, 128)), shape((256, 1536)), shape((256, 512), F32),
             shape((16, 2, 16, 256)), shape((16, 2, 16, 256)), shape((16, 128)),
         ),
-        in_specs=[SMEM] + [VMEM] * 10,
-        out_specs=(VMEM,) * 6,
-        scratch_shapes=[pltpu.VMEM((256, 512), BF16)] * 2,
+        in_specs=[SMEM] + [VMEM] * 9,
+        out_specs=(VMEM,) * 8,
+        scratch_shapes=[
+            pltpu.VMEM((256, 512), BF16),
+            pltpu.VMEM((256, 1024), BF16),
+            pltpu.VMEM((256, 512), BF16),
+            pltpu.VMEM((256, 1024), F32),
+            pltpu.VMEM((256, 1536), F32),
+            pltpu.VMEM((256, 512), BF16),
+            pltpu.VMEM((256, 512), BF16),
+        ],
         compiler_params=PARAMS,
         name="window_backward",
-    )(place, xw, dyw, w_qkv, w_out, cosine, sine, normed, qk, value, scales)
+    )(place, diag, east, below, own, gain_row, w_qkv, w_out, cosine, sine)
 
     got = lax.ppermute(give, "c", [(0, 1), (1, 0)])
     keep = pl.pallas_call(

time: 63.1 us -> 62.9 us (level)
    pallas_call x2 -> x1, Pallas kernels: 6.07 us -> 5.89 us  [per_device(): pl.pallas_call(window_kernel, out_shape=(shape((256, 512)), shape((256, 5...]
where the time goes in v3:
time: 62.9 us; the launch traced here: 62.3 us
  blocking collectives  18.7 us (30%)
  starting transfers between devices  17.4 us (28%)
  waiting for transfers between devices  12.5 us (20%)
  Pallas kernels  11.8 us (19%)
  other arithmetic  1.18 us (2%)
  between operations  0.74 us (1%)
    all_to_all x1, blocking collectives, per_device(): parts = lax.all_to_all(parts, ('yh', 'yl', 'z'), 0, 0, tiled=True)  18.7 us
    ppermute x6, starting transfers between devices, send(): return lax.ppermute(v, every, pairs)  11.9 us
    ppermute x4, waiting for transfers between devices, along_x(): return lax.ppermute(v, 'x', [(i, i ^ mask) for i in range(4)])  8.04 us
    pallas_call x1, Pallas kernels, per_device(): pl.pallas_call(window_kernel, out_shape=(shape((256, 512)), shape((256, 5...  5.89 us
    ppermute x4, starting transfers between devices, along_x(): return lax.ppermute(v, 'x', [(i, i ^ mask) for i in range(4)])  5.37 us
    ppermute x6, waiting for transfers between devices, send(): return lax.ppermute(v, every, pairs)  2.95 us
    pallas_call x1, Pallas kernels, per_device(): pl.pallas_call(fetch_kernel, out_shape=(shape((512, 1536)), shape((512, 5...  1.54 us
    ppermute x1, waiting for transfers between devices, per_device(): got = lax.ppermute(give, 'c', [(0, 1), (1, 0)])  1.48 us
  transfers between devices with their start and end apart: 11, of which 6 were waited for; matrix products, arithmetic and copies ran while one was open for 2% of the time, Pallas kernels for 5%

profile of v3, /device:TPU:6, one launch (start us, length us, event | category | flops | bytes accessed | tf_op | source)
XLA Modules:
  0.0 62.3 jit_solution(11527104750065167046)
XLA Ops:
  0.6 1.1 %quads.1 = (bf16[2,4,4,4,512]{4,3,2,1,0:T(4,128)(2,1)S(1)}, bf16[2,4,4,4,512]{4,3,2,1,0:T(4,128)(2,1)S(1)}, bf16[2,4,4,4,512]{4,3,2,1,0:T(4,128)(2,1)S(1)}, bf16[2,4,4,4,512]{4,3,2,1,0:T(4,128)(2,1)S(1)}) custom-call(bf16[4,8,8,512]{3,2,1,0:T(8,128)(2,1)} %x_ref.1, bf16[4,8,8,512]{3,2,1,0:T(8,128)(2,1)} %dy_ref.1), custom_call_target="tpu_custom_call" | custom-call | tf_op jit(solution)/shard_map/quads/pallas_call | solution.py:321
  1.8 8.1 %collective-permute-start = (bf16[2,4,4,4,512]{4,3,2,1,0:T(4,128)(2,1)S(1)}, bf16[2,4,4,4,512]{4,3,2,1,0:T(4,128)(2,1)S(1)}, u32[]{:S(2)}, u32[]{:S(2)}) collective-permute-start(bf16[2,4,4,4,512]{4,3,2,1,0:T(4,128)(2,1)S(1)} %get-tuple-element.38), channel_id=1, source_target_pairs={{0,255},{1,248},{2,249},{3,250},{4,251},{5,252},{6,253},{7,254},{8... | collective-permute-start | bytes 393224 | tf_op jit(solution)/shard_map/ppermute | solution.py:319
  9.9 1.7 %collective-permute-start.1 = (bf16[2,4,4,4,512]{4,3,2,1,0:T(4,128)(2,1)S(1)}, bf16[2,4,4,4,512]{4,3,2,1,0:T(4,128)(2,1)S(1)}, u32[]{:S(2)}, u32[]{:S(2)}) collective-permute-start(bf16[2,4,4,4,512]{4,3,2,1,0:T(4,128)(2,1)S(1)} %get-tuple-element.39), channel_id=1, source_target_pairs={{0,248},{1,249},{2,250},{3,251},{4,252},{5,253},{6,254},{7,255},{8... | collective-permute-start | bytes 393224 | tf_op jit(solution)/shard_map/ppermute | solution.py:319
  11.6 0.1 collective-permute-start.2
  11.8 0.2 sine_multiply_fusion
  12.0 0.0 copy-start
  12.0 1.5 %fetch_weights.1 = (bf16[512,1536]{1,0:T(8,128)(2,1)S(1)}, bf16[512,512]{1,0:T(8,128)(2,1)S(1)}) custom-call(bf16[512,1536]{1,0:T(8,128)(2,1)} %wqkv_ref.1, bf16[512,512]{1,0:T(8,128)(2,1)} %wout_ref.1), custom_call_target="tpu_custom_call" | custom-call | bytes 4000000 | tf_op jit(solution)/shard_map/fetch_weights/pallas_call | solution.py:331
  13.6 0.1 pad_add_fusion.place
  13.6 0.0 collective-permute-done.diag_ref
  13.6 0.5 collective-permute-done.1.east_ref
  14.1 2.4 %collective-permute-done.2.below_ref = bf16[2,4,4,4,512]{4,3,2,1,0:T(4,128)(2,1)S(1)} collective-permute-done((bf16[2,4,4,4,512]{4,3,2,1,0:T(4,128)(2,1)S(1)}, bf16[2,4,4,4,512]{4,3,2,1,0:T(4,128)(2,1)S(1)}, u32[]{:S(2)}, u32[]{:S(2)}) %collective-permute-start.2) | collective-permute-done | bytes 131104 | tf_op jit(solution)/shard_map/ppermute | solution.py:319
  16.6 0.0 copy-done
  16.6 5.9 %window_backward.1 = (bf16[256,512]{1,0:T(8,128)(2,1)S(1)}, bf16[256,512]{1,0:T(8,128)(2,1)S(1)}, bf16[4,1040,128]{2,1,0:T(8,128)(2,1)S(1)}, bf16[256,1536]{1,0:...) custom-call(s32[4]{0:T(128)S(1)} %pad_add_fusion.place, ...), custom_call_target="tpu_custom_call" | custom-call | tf_op jit(solution)/shard_map/window_backward/pallas_call | solution.py:353
  22.5 0.1 collective-permute-start.3
  22.6 1.2 %kept_half.1.keep_ref = bf16[4,1040,128]{2,1,0:T(8,128)(2,1)S(1)} custom-call(s32[4]{0:T(128)S(1)} %pad_add_fusion.place, bf16[256,512]{1,0:T(8,128)(2,1)S(1)} %get-tuple-element.44.dy_ref, bf16[256,1536]{1,0:T(8,128)(2,1)S(1)} %get-tuple-element.45.dqkv_ref, bf16[16,2,16,256]{3,2,1,0:T(8,128)(2,1)S(1)} %get-tuple-element.46.nt_ref, ...), custom_call_target="tpu_custom_call" | custom-call | flops 300000000 | bytes 4000000 | tf_op jit(solution)/shard_map/kept_half/pallas_call | solution.py:376
  23.8 1.5 %collective-permute-done.3.got_ref = bf16[4,1040,128]{2,1,0:T(8,128)(2,1)S(1)} collective-permute-done((bf16[4,1040,128]{2,1,0:T(8,128)(2,1)S(1)}, bf16[4,1040,128]{2,1,0:T(8,128)(2,1)S(1)}, u32[]{:S(2)}, u32[]{:S(2)}) %collective-permute-start.3) | collective-permute-done | bytes 1064992 | tf_op jit(solution)/shard_map/ppermute | solution.py:375
  25.2 0.3 pair_sum.1
  25.5 0.0 copy-start.1
  25.5 0.6 collective-permute-start.4
  26.1 2.0 %collective-permute-start.5 = (bf16[2,512,128]{2,1,0:T(8,128)(2,1)S(1)}, bf16[2,512,128]{2,1,0:T(8,128)(2,1)S(1)}, u32[]{:S(2)}, u32[]{:S(2)}) collective-permute-start(bf16[2,512,128]{2,1,0:T(8,128)(2,1)S(1)} %get-tuple-element.56), channel_id=1, source_target_pairs={{0,6},{2,4},{4,2},{6,0},{1,7},{3,5},{5,3},{7,1},{8,14},{10,12},{12... | collective-permute-start | bytes 786440 | tf_op jit(solution)/shard_map/ppermute | solution.py:386
  28.1 0.2 norm_backward.1
  28.4 0.1 collective-permute-start.8
  28.4 1.9 %collective-permute-start.9 = (bf16[4,4,4,512]{3,2,1,0:T(4,128)(2,1)S(1)}, bf16[4,4,4,512]{3,2,1,0:T(4,128)(2,1)S(1)}, u32[]{:S(2)}, u32[]{:S(2)}) collective-permute-start(bf16[4,4,4,512]{3,2,1,0:T(4,128)(2,1)S(1)} %get-tuple-element.64), channel_id=1, source_target_pairs={{0,1},{1,2},{2,3},{3,4},{4,5},{5,6},{6,7},{7,0},{8,9},{9,10},{10,1... | collective-permute-start | bytes 196616 | tf_op jit(solution)/shard_map/ppermute | solution.py:319
  30.3 0.0 collective-permute-start.10
  30.3 5.1 %collective-permute-done.5.b_got = bf16[2,512,128]{2,1,0:T(8,128)(2,1)S(1)} collective-permute-done((bf16[2,512,128]{2,1,0:T(8,128)(2,1)S(1)}, bf16[2,512,128]{2,1,0:T(8,128)(2,1)S(1)}, u32[]{:S(2)}, u32[]{:S(2)}) %collective-permute-start.5) | collective-permute-done | bytes 262176 | tf_op jit(solution)/shard_map/ppermute | solution.py:386
  35.4 0.0 collective-permute-done.4.a_got
  35.4 0.1 first_x_sum.1
  35.6 0.4 collective-permute-start.7
  36.0 2.3 %collective-permute-start.6 = (bf16[528,128]{1,0:T(8,128)(2,1)S(1)}, bf16[528,128]{1,0:T(8,128)(2,1)S(1)}, u32[]{:S(2)}, u32[]{:S(2)}) collective-permute-start(bf16[528,128]{1,0:T(8,128)(2,1)S(1)} %get-tuple-element.58), channel_id=1, source_target_pairs={{0,6},{2,4},{4,2},{6,0},{1,7},{3,5},{5,3},{7,1},{8,14},{10,12},{12... | collective-permute-start | bytes 405512 | tf_op jit(solution)/shard_map/ppermute | solution.py:386
  38.3 0.0 collective-permute-done.8
  38.3 0.0 collective-permute-done.9
  38.4 0.0 collective-permute-done.10
  38.4 0.0 copy-done.1
  38.4 0.9 %add_convert_fusion = bf16[4,8,8,512]{3,2,1,0:T(8,128)(2,1)} fusion(bf16[4,8,8,512]{3,2,1,0:T(8,128)(2,1)S(1)} %copy-done.1, bf16[4,4,4,512]{3,2,1,0:T(4,128)(2,1)S(1)} %get-tuple-element.66, bf16[4,4,4,512]{3,2,1,0:T(4,128)(2,1)S(1)} %collective-permute-done.10, bf16[4,4,4,512]{3,2,1,0:T(4,128)(2,1)S(1)} %collective-permute-done.9, ...), kind=kLoop, calls=%fused_computation | loop fusion | flops 1441792 | bytes 786432 | tf_op jit(solution)/shard_map/convert_element_type | solution.py:410
  39.2 1.4 %collective-permute-done.7.b_got = bf16[512,128]{1,0:T(8,128)(2,1)S(1)} collective-permute-done((bf16[512,128]{1,0:T(8,128)(2,1)S(1)}, bf16[512,128]{1,0:T(8,128)(2,1)S(1)}, u32[]{:S(2)}, u32[]{:S(2)}) %collective-permute-start.7) | collective-permute-done | bytes 131104 | tf_op jit(solution)/shard_map/ppermute | solution.py:386
  40.6 1.6 %collective-permute-done.6.a_got = bf16[528,128]{1,0:T(8,128)(2,1)S(1)} collective-permute-done((bf16[528,128]{1,0:T(8,128)(2,1)S(1)}, bf16[528,128]{1,0:T(8,128)(2,1)S(1)}, u32[]{:S(2)}, u32[]{:S(2)}) %collective-permute-start.6) | collective-permute-done | bytes 135200 | tf_op jit(solution)/shard_map/ppermute | solution.py:386
  42.2 0.1 second_x_sum.1
  42.3 18.7 %all_to_all.5.in_ref = bf16[32,9,4,128]{3,2,1,0:T(4,128)(2,1)S(1)} all-to-all(bf16[32,9,4,128]{3,2,1,0:T(4,128)(2,1)S(1)} %second_x_sum.1), channel_id=1, replica_groups=mesh['z'=8,'yh'=2,'c'=2,'x'=4,'yl'=2] {'yh','yl','z'}, dimensions={0} | all-to-all | bytes 589824 | tf_op jit(solution)/shard_map/all_to_all | solution.py:428
  61.0 1.3 %last_sum.1 = (f32[16,192]{1,0:T(8,128)}, f32[16,64]{1,0:T(8,128)}, f32[4,128]{1,0:T(4,128)}) custom-call(s32[4]{0:T(128)S(1)} %pad_add_fusion.place, bf16[32,9,4,128]{3,2,1,0:T(4,128)(2,1)S(1)} %all_to_all.5.in_ref), custom_call_target="tpu_custom_call" | custom-call | tf_op jit(solution)/shard_map/last_sum/pallas_call | solution.py:429
  (3 shorter events, 0.0 us)
Async XLA Ops:
  1.8 11.9 %collective-permute-start = (bf16[2,4,4,4,512]{4,3,2,1,0:T(4,128)(2,1)S(1)}, bf16[2,4,4,4,512]{4,3,2,1,0:T(4,128)(2,1)S(1)}, u32[]{:S(2)}, u32[]{:S(2)}) collective-permute-start(bf16[2,4,4,4,512]{4,3,2,1,0:T(4,128)(2,1)S(1)} %get-tuple-element.38), channel_id=1, source_target_pairs={{0,255},{1,248},{2,249},{3,250},{4,251},{5,252},{6,253},{7,254},{8... | collective-permute-start | bytes 393224 | tf_op jit(solution)/shard_map/ppermute | solution.py:319
  9.9 4.3 %collective-permute-start.1 = (bf16[2,4,4,4,512]{4,3,2,1,0:T(4,128)(2,1)S(1)}, bf16[2,4,4,4,512]{4,3,2,1,0:T(4,128)(2,1)S(1)}, u32[]{:S(2)}, u32[]{:S(2)}) collective-permute-start(bf16[2,4,4,4,512]{4,3,2,1,0:T(4,128)(2,1)S(1)} %get-tuple-element.39), channel_id=1, source_target_pairs={{0,248},{1,249},{2,250},{3,251},{4,252},{5,253},{6,254},{7,255},{8... | collective-permute-start | bytes 393224 | tf_op jit(solution)/shard_map/ppermute | solution.py:319
  11.6 5.0 %collective-permute-start.2 = (bf16[2,4,4,4,512]{4,3,2,1,0:T(4,128)(2,1)S(1)}, bf16[2,4,4,4,512]{4,3,2,1,0:T(4,128)(2,1)S(1)}, u32[]{:S(2)}, u32[]{:S(2)}) collective-permute-start(bf16[2,4,4,4,512]{4,3,2,1,0:T(4,128)(2,1)S(1)} %get-tuple-element.40), channel_id=1, source_target_pairs={{0,7},{1,0},{2,1},{3,2},{4,3},{5,4},{6,5},{7,6},{8,15},{9,8},{10,9... | collective-permute-start | bytes 393224 | tf_op jit(solution)/shard_map/ppermute | solution.py:319
  12.0 4.6 %copy-start = (f32[512]{0:T(512)S(1)}, f32[512]{0:T(512)}, u32[]{:S(2)}) copy-start(f32[512]{0:T(512)} %param.7) | copy-start | bytes 6148
  22.5 2.8 %collective-permute-start.3 = (bf16[4,1040,128]{2,1,0:T(8,128)(2,1)S(1)}, bf16[4,1040,128]{2,1,0:T(8,128)(2,1)S(1)}, u32[]{:S(2)}, u32[]{:S(2)}) collective-permute-start(bf16[4,1040,128]{2,1,0:T(8,128)(2,1)S(1)} %get-tuple-element.49), channel_id=1, source_target_pairs={{0,8},{8,0},{1,9},{9,1},{2,10},{10,2},{3,11},{11,3},{4,12},{12,4},... | collective-permute-start | bytes 3194888 | tf_op jit(solution)/shard_map/ppermute | solution.py:375
  25.5 12.9 %copy-start.1 = (bf16[4,8,8,512]{3,2,1,0:T(8,128)(2,1)S(1)}, bf16[4,8,8,512]{3,2,1,0:T(8,128)(2,1)}, u32[]{:S(2)}) copy-start(bf16[4,8,8,512]{3,2,1,0:T(8,128)(2,1)} %dy_ref.1) | copy-start | bytes 786436
  25.5 9.9 %collective-permute-start.4 = (bf16[2,528,128]{2,1,0:T(8,128)(2,1)S(1)}, bf16[2,528,128]{2,1,0:T(8,128)(2,1)S(1)}, u32[]{:S(2)}, u32[]{:S(2)}) collective-permute-start(bf16[2,528,128]{2,1,0:T(8,128)(2,1)S(1)} %get-tuple-element.54), channel_id=1, source_target_pairs={{0,2},{2,0},{4,6},{6,4},{1,3},{3,1},{5,7},{7,5},{8,10},{10,8},{12,... | collective-permute-start | bytes 811016 | tf_op jit(solution)/shard_map/ppermute | solution.py:386
  26.1 9.3 %collective-permute-start.5 = (bf16[2,512,128]{2,1,0:T(8,128)(2,1)S(1)}, bf16[2,512,128]{2,1,0:T(8,128)(2,1)S(1)}, u32[]{:S(2)}, u32[]{:S(2)}) collective-permute-start(bf16[2,512,128]{2,1,0:T(8,128)(2,1)S(1)} %get-tuple-element.56), channel_id=1, source_target_pairs={{0,6},{2,4},{4,2},{6,0},{1,7},{3,5},{5,3},{7,1},{8,14},{10,12},{12... | collective-permute-start | bytes 786440 | tf_op jit(solution)/shard_map/ppermute | solution.py:386
  28.4 10.0 %collective-permute-start.8 = (bf16[4,4,4,512]{3,2,1,0:T(4,128)(2,1)S(1)}, bf16[4,4,4,512]{3,2,1,0:T(4,128)(2,1)S(1)}, u32[]{:S(2)}, u32[]{:S(2)}) collective-permute-start(bf16[4,4,4,512]{3,2,1,0:T(4,128)(2,1)S(1)} %get-tuple-element.63), channel_id=1, source_target_pairs={{0,9},{1,10},{2,11},{3,12},{4,13},{5,14},{6,15},{7,8},{8,17},{9,18... | collective-permute-start | bytes 196616 | tf_op jit(solution)/shard_map/ppermute | solution.py:319
  28.4 9.9 %collective-permute-start.9 = (bf16[4,4,4,512]{3,2,1,0:T(4,128)(2,1)S(1)}, bf16[4,4,4,512]{3,2,1,0:T(4,128)(2,1)S(1)}, u32[]{:S(2)}, u32[]{:S(2)}) collective-permute-start(bf16[4,4,4,512]{3,2,1,0:T(4,128)(2,1)S(1)} %get-tuple-element.64), channel_id=1, source_target_pairs={{0,1},{1,2},{2,3},{3,4},{4,5},{5,6},{6,7},{7,0},{8,9},{9,10},{10,1... | collective-permute-start | bytes 196616 | tf_op jit(solution)/shard_map/ppermute | solution.py:319
  30.3 8.0 %collective-permute-start.10 = (bf16[4,4,4,512]{3,2,1,0:T(4,128)(2,1)S(1)}, bf16[4,4,4,512]{3,2,1,0:T(4,128)(2,1)S(1)}, u32[]{:S(2)}, u32[]{:S(2)}) collective-permute-start(bf16[4,4,4,512]{3,2,1,0:T(4,128)(2,1)S(1)} %get-tuple-element.65), channel_id=1, source_target_pairs={{0,8},{1,9},{2,10},{3,11},{4,12},{5,13},{6,14},{7,15},{8,16},{9,17... | collective-permute-start | bytes 196616 | tf_op jit(solution)/shard_map/ppermute | solution.py:319
  35.6 5.1 %collective-permute-start.7 = (bf16[512,128]{1,0:T(8,128)(2,1)S(1)}, bf16[512,128]{1,0:T(8,128)(2,1)S(1)}, u32[]{:S(2)}, u32[]{:S(2)}) collective-permute-start(bf16[512,128]{1,0:T(8,128)(2,1)S(1)} %get-tuple-element.60), channel_id=1, source_target_pairs={{0,2},{2,0},{4,6},{6,4},{1,3},{3,1},{5,7},{7,5},{8,10},{10,8},{12,... | collective-permute-start | bytes 393224 | tf_op jit(solution)/shard_map/ppermute | solution.py:386
  36.0 6.2 %collective-permute-start.6 = (bf16[528,128]{1,0:T(8,128)(2,1)S(1)}, bf16[528,128]{1,0:T(8,128)(2,1)S(1)}, u32[]{:S(2)}, u32[]{:S(2)}) collective-permute-start(bf16[528,128]{1,0:T(8,128)(2,1)S(1)} %get-tuple-element.58), channel_id=1, source_target_pairs={{0,6},{2,4},{4,2},{6,0},{1,7},{3,5},{5,3},{7,1},{8,14},{10,12},{12... | collective-permute-start | bytes 405512 | tf_op jit(solution)/shard_map/ppermute | solution.py:386
